TPU v7x, 32 devices: a whole 2x2x4 slice. The times are simulated.
32 devices in a mesh: dp: 8 (over z, x), pipe: 4 (over y, core).
Axes of the slice: x: 2, y: 2, z: 4, core: 2. Of those that a mesh axis runs over, the one named last changes fastest.
Arguments:
- inputs: bfloat16 [24, 256, 768], P('dp', 'pipe'), may hold values from -6 to 6
- lengths: int32 [24], P('dp'), may hold values from 32 to 256, as said below
- w_qkv: bfloat16 [768, 2304], replicated, may hold values from -0.21875 to 0.21875
- w_out: bfloat16 [768, 768], replicated, may hold values from -0.875 to 0.875
- w_up: bfloat16 [768, 3072], replicated, may hold values from -0.21875 to 0.21875
- w_down: bfloat16 [3072, 768], replicated, may hold values from -0.109375 to 0.109375
- norm1_gain: float32 [768], replicated, may hold values from 0.1 to 1.9
- norm1_shift: float32 [768], replicated, may hold values from -3 to 3
- norm2_gain: float32 [768], replicated, may hold values from 0.1 to 1.9
- norm2_shift: float32 [768], replicated, may hold values from -3 to 3
- pass_embed: float32 [768], replicated, may hold values from -3 to 3
- cotangent: bfloat16 [24, 256, 768], P('dp', 'pipe'), may hold values from -6 to 6
Outputs:
- block_out: bfloat16 [24, 256, 768], P('dp', 'pipe')
- input_grads: bfloat16 [24, 256, 768], P('dp', 'pipe')
- grad_qkv: float32 [768, 2304], P('pipe')
- grad_out: float32 [768, 768], P('pipe')
- grad_up: float32 [768, 3072], P('pipe')
- grad_down: float32 [3072, 768], P('pipe')
- grad_norm1_gain: float32 [768], P('pipe')
- grad_norm1_shift: float32 [768], P('pipe')
- grad_norm2_gain: float32 [768], P('pipe')
- grad_norm2_shift: float32 [768], P('pipe')
- grad_pass_embed: float32 [768], P('pipe')
Inputs may be any that keep to these rules, and one draw needn't show every extreme that they name: `lengths`: in each aligned group of 3 sequences, one has length 256.
All inputs are finite; a program needn't handle non-finite values.
Results may differ from a plain program's by a relative error of at most 0.018.
Values may be sent and summed in bfloat16 or wider, within the bound.
A program may use at most 320 MiB of HBM per device.

v0:
```python
import jax
import jax.numpy as jnp
from jax import lax
from jax.sharding import PartitionSpec as P

HEADS = 12
HEAD = 64


def layer_norm(values, gain, shift):
    center = values - jnp.mean(values, axis=-1, keepdims=True)
    spread = jnp.mean(center * center, axis=-1, keepdims=True)
    return center * lax.rsqrt(spread + 1e-05) * gain + shift


def matmul(left, right):
    return jnp.dot(left, right, preferred_element_type=jnp.float32)


def left_product(left, right):
    return lax.dot_general(
        left, right, (((0,), (0,)), ((), ())), preferred_element_type=jnp.float32
    )


def right_product(left, right):
    return lax.dot_general(
        left, right, (((1,), (1,)), ((), ())), preferred_element_type=jnp.float32
    )


def smooth(values):
    return jax.nn.gelu(values, approximate=True)


def mask_for(length, seq_len):
    places = jnp.arange(seq_len)
    inside = places < length
    causal = (places[None, :] <= places[:, None]) & inside[None, :]
    return (causal, inside.astype(jnp.float32)[:, None])


def split_heads(values):
    return values.reshape(values.shape[0], HEADS, HEAD)


def attend(queries, key_rows, value_rows, allowed):
    scores = jnp.einsum(
        "qhd,khd->hqk",
        split_heads(queries),
        split_heads(key_rows),
        preferred_element_type=jnp.float32,
    ) * HEAD ** (-0.5)
    scores = jnp.where(allowed[None], scores, -1e30)
    row_max = jnp.max(scores, axis=-1, keepdims=True)
    weights = jnp.exp(scores - row_max)
    row_total = jnp.sum(weights, axis=-1, keepdims=True)
    soft = (weights / row_total).astype(jnp.bfloat16)
    context = jnp.einsum(
        "hqk,khd->qhd", soft, split_heads(value_rows), preferred_element_type=jnp.float32
    )
    return (
        context.reshape(queries.shape[0], -1).astype(jnp.bfloat16),
        row_max + jnp.log(row_total),
    )


def attend_back(queries, key_rows, value_rows, log_total, d_context, allowed):
    q_heads = split_heads(queries)
    k_heads = split_heads(key_rows)
    v_heads = split_heads(value_rows)
    d_heads = split_heads(d_context)
    scale = HEAD ** (-0.5)
    scores = (
        jnp.einsum("qhd,khd->hqk", q_heads, k_heads, preferred_element_type=jnp.float32) * scale
    )
    scores = jnp.where(allowed[None], scores, -1e30)
    soft = jnp.exp(scores - log_total)
    d_values = jnp.einsum(
        "hqk,qhd->khd", soft.astype(jnp.bfloat16), d_heads, preferred_element_type=jnp.float32
    )
    d_soft = jnp.einsum("qhd,khd->hqk", d_heads, v_heads, preferred_element_type=jnp.float32)
    d_scores = (soft * (d_soft - jnp.sum(d_soft * soft, axis=-1, keepdims=True))).astype(
        jnp.bfloat16
    )
    d_queries = (
        jnp.einsum("hqk,khd->qhd", d_scores, k_heads, preferred_element_type=jnp.float32) * scale
    )
    d_keys = (
        jnp.einsum("hqk,qhd->khd", d_scores, q_heads, preferred_element_type=jnp.float32) * scale
    )
    return (
        d_queries.reshape(queries.shape[0], -1),
        d_keys.reshape(key_rows.shape[0], -1),
        d_values.reshape(value_rows.shape[0], -1),
    )


def forward_block(state, weights, extra_keys, extra_values, allowed):
    w_qkv, w_out, w_up, w_down, gain_one, shift_one, gain_two, shift_two = weights
    features = state.shape[1]
    normed = layer_norm(state, gain_one, shift_one).astype(jnp.bfloat16)
    qkv = matmul(normed, w_qkv).astype(jnp.bfloat16)
    queries = qkv[:, :features]
    key_new = qkv[:, features : 2 * features]
    value_new = qkv[:, 2 * features :]
    if extra_keys is None:
        key_rows, value_rows = (key_new, value_new)
    else:
        key_rows = jnp.concatenate([extra_keys, key_new], axis=0)
        value_rows = jnp.concatenate([extra_values, value_new], axis=0)
    context, log_total = attend(queries, key_rows, value_rows, allowed)
    residual = state + matmul(context, w_out)
    normed_two = layer_norm(residual, gain_two, shift_two).astype(jnp.bfloat16)
    hidden = matmul(normed_two, w_up)
    active = smooth(hidden).astype(jnp.bfloat16)
    result = residual + matmul(active, w_down)
    saved = (
        state,
        normed,
        queries,
        key_rows,
        value_rows,
        log_total,
        context,
        residual,
        normed_two,
        hidden,
        active,
    )
    return (result, key_new, value_new, saved)


def backward_block(grad_result, weights, saved, allowed, more_keys, more_values):
    w_qkv, w_out, w_up, w_down, gain_one, shift_one, gain_two, shift_two = weights
    (
        state,
        normed,
        queries,
        key_rows,
        value_rows,
        log_total,
        context,
        residual,
        normed_two,
        hidden,
        active,
    ) = saved
    d_branch = grad_result.astype(jnp.bfloat16)
    g_down = left_product(active, d_branch)
    d_active = right_product(d_branch, w_down)
    smooth_value, smooth_back = jax.vjp(smooth, hidden)
    d_hidden = smooth_back(d_active)[0].astype(jnp.bfloat16)
    g_up = left_product(normed_two, d_hidden)
    d_normed_two = right_product(d_hidden, w_up)
    norm_value, norm_back = jax.vjp(layer_norm, residual, gain_two, shift_two)
    d_residual, g_gain_two, g_shift_two = norm_back(d_normed_two)
    d_residual = grad_result + d_residual
    d_attention = d_residual.astype(jnp.bfloat16)
    g_out = left_product(context, d_attention)
    d_context = right_product(d_attention, w_out).astype(jnp.bfloat16)
    d_queries, d_keys, d_values = attend_back(
        queries, key_rows, value_rows, log_total, d_context, allowed
    )
    row_count = state.shape[0]
    d_qkv = jnp.concatenate(
        [d_queries, d_keys[-row_count:] + more_keys, d_values[-row_count:] + more_values], axis=1
    ).astype(jnp.bfloat16)
    g_qkv = left_product(normed, d_qkv)
    d_normed = right_product(d_qkv, w_qkv)
    first_value, first_back = jax.vjp(layer_norm, state, gain_one, shift_one)
    d_state, g_gain_one, g_shift_one = first_back(d_normed)
    grads = (g_qkv, g_out, g_up, g_down, g_gain_one, g_shift_one, g_gain_two, g_shift_two)
    return (d_residual + d_state, grads, d_keys[:-row_count], d_values[:-row_count])


def weight_zeros(weights):
    return tuple((jnp.zeros(array.shape, jnp.float32) for array in weights))


def shards(
    inputs,
    lengths,
    w_qkv,
    w_out,
    w_up,
    w_down,
    norm1_gain,
    norm1_shift,
    norm2_gain,
    norm2_shift,
    pass_embed,
    cotangent,
):
    section_index = lax.axis_index("pipe")
    sections = lax.axis_size("pipe")
    weights = (w_qkv, w_out, w_up, w_down, norm1_gain, norm1_shift, norm2_gain, norm2_shift)
    gathered = lax.all_gather(inputs, "pipe", axis=1, tiled=True)
    seq_len = gathered.shape[1]
    features = gathered.shape[2]
    own_slot = jnp.maximum(section_index - 1, 0)
    padded_cot = jnp.concatenate([jnp.zeros_like(cotangent[:1]), cotangent], axis=0)
    own_cot = lax.all_to_all(padded_cot, "pipe", split_axis=0, concat_axis=1, tiled=True)[0]
    own_length = lax.dynamic_index_in_dim(lengths, own_slot, 0, keepdims=False)
    allowed_own, inside_own = mask_for(own_length, seq_len)
    allowed_both = jnp.concatenate([allowed_own, allowed_own], axis=1)

    def both_passes(unused):
        state = lax.dynamic_index_in_dim(gathered, own_slot, 0, keepdims=False).astype(jnp.float32)
        first, key_first, value_first, saved_first = forward_block(
            state, weights, None, None, allowed_own
        )
        second_in = first.astype(jnp.bfloat16).astype(jnp.float32) + pass_embed
        result, key_unused, value_unused, saved_second = forward_block(
            second_in, weights, key_first, value_first, allowed_both
        )
        grad_result = own_cot.astype(jnp.float32) * inside_own
        empty = jnp.zeros((seq_len, features), jnp.float32)
        d_carry, grads_two, d_keys, d_values = backward_block(
            grad_result, weights, saved_second, allowed_both, empty, empty
        )
        carried_grad = d_carry.astype(jnp.bfloat16).astype(jnp.float32)
        d_state, grads_one, keys_unused, values_unused = backward_block(
            carried_grad, weights, saved_first, allowed_own, d_keys, d_values
        )
        summed_grads = tuple(
            (first_term + second_term for first_term, second_term in zip(grads_one, grads_two))
        )
        return (result * inside_own, d_carry, summed_grads, d_state.astype(jnp.bfloat16))

    def both_zeros(unused):
        rows_high = jnp.zeros((seq_len, features), jnp.float32)
        return (
            rows_high,
            rows_high,
            weight_zeros(weights),
            jnp.zeros((seq_len, features), jnp.bfloat16),
        )

    second_out, d_second, grads_both, d_state_own = lax.cond(
        section_index > 0, both_passes, both_zeros, 0
    )
    received_grads = lax.all_to_all(
        d_state_own[None], "pipe", split_axis=1, concat_axis=0, tiled=True
    )
    input_grads = received_grads[1:]
    received_out = lax.all_to_all(
        second_out.astype(jnp.bfloat16)[None], "pipe", split_axis=1, concat_axis=0, tiled=True
    )
    block_out = received_out[1:]
    grad_all = tuple(grads_both) + (jnp.sum(d_second, axis=0),)
    summed = lax.psum(grad_all, ("dp", "pipe"))
    grads_final = tuple(
        (
            lax.dynamic_slice_in_dim(
                array, section_index * (array.shape[0] // sections), array.shape[0] // sections, 0
            )
            for array in summed
        )
    )
    return (block_out, input_grads) + tuple(grads_final)


def solution(mesh):
    placed = (
        P("dp", "pipe", None),
        P("dp"),
        P(),
        P(),
        P(),
        P(),
        P(),
        P(),
        P(),
        P(),
        P(),
        P("dp", "pipe", None),
    )
    return jax.shard_map(
        shards,
        mesh=mesh,
        in_specs=placed,
        out_specs=(
            P("dp", "pipe", None),
            P("dp", "pipe", None),
            P("pipe", None),
            P("pipe", None),
            P("pipe", None),
            P("pipe", None),
            P("pipe"),
            P("pipe"),
            P("pipe"),
            P("pipe"),
            P("pipe"),
        ),
        check_vma=False,
    )
```

profile of v0, /device:TPU:0, one launch (start us, length us, event | category | flops | bytes accessed | tf_op | source)
XLA Modules:
  0.0 609.9 jit_solution(1780948506062846405)
XLA Ops:
  7.9 1.7 concatenate.21
  9.6 4.2 all-to-all-start
  13.9 1.2 dynamic_slice.35
  17.4 3.9 all-to-all-done
  21.3 8.4 %all-gather.2.cloned.1.call-done = bf16[3,256,768]{2,1,0:T(8,128)(2,1)} async-done(((bf16[3,64,768]{2,1,0:T(8,128)(2,1)}), bf16[3,256,768]{2,1,0:T(8,128)(2,1)}) %all-gather.2.cloned.1.call-update) | async-done | bytes 1179664 | tf_op jit(solution)/shard_map/all_gather | solution.py:198
  29.8 18.9 %conditional.1 = (f32[256,768]{1,0:T(8,128)}, f32[256,768]{1,0:T(8,128)}, f32[768,2304]{1,0:T(8,128)}, f32[768,768]{1,0:T(8,128)}, f32[768,3072]{1,0:T(8,128)}, ...) conditional(s32[]{:T(128)} %convert_element_type.127, () %tuple.16, ...), branch_computations={%region_0.1_spmd, %region_1.32_spmd} | conditional | flops 23715633152 | bytes 729739840 | solution.py:240
  29.8 4.7 broadcast.201
  34.5 4.3 broadcast.202
  38.8 3.3 broadcast.199
  42.1 1.6 broadcast.200
  48.7 1.2 convert_bitcast_fusion.1
  51.0 3.0 reduce.2
  54.8 110.9 %all-to-all-start.1 = ((bf16[4,2,24576]{2,1,0:T(2,128)(2,1)}), bf16[4,2,24576]{2,1,0:T(2,128)(2,1)S(1)}, u32[]{:S(2)}, u32[]{:S(2)}) async-start(bf16[4,2,24576]{2,1,0:T(2,128)(2,1)} %reshape.259), calls=%async_computation.1 | async-start | bytes 786432 | tf_op jit(solution)/shard_map/all_to_all | solution.py:247
  165.8 1.6 copy.106
  167.4 3.0 reduce.1
  171.2 6.7 %all-to-all-done.1 = bf16[4,2,24576]{2,1,0:T(2,128)(2,1)S(1)} async-done(((bf16[4,2,24576]{2,1,0:T(2,128)(2,1)}), bf16[4,2,24576]{2,1,0:T(2,128)(2,1)S(1)}, u32[]{:S(2)}, u32[]{:S(2)}) %all-to-all-start.1) | async-done | bytes 393248 | tf_op jit(solution)/shard_map/all_to_all | solution.py:247
  177.9 3.5 all-to-all-start.2
  181.4 1.2 reduce_sum.253
  182.6 45.8 %all-reduce.1 = (f32[768]{0:T(1024)S(1)}, f32[768]{0:T(1024)S(1)}, f32[768]{0:T(1024)S(1)}, f32[768]{0:T(1024)S(1)}, f32[768]{0:T(1024)S(1)}) all-reduce(f32[768]{0:T(1024)} %get-tuple-element.74, f32[768]{0:T(1024)} %get-tuple-element.75, f32[768]{0:T(1024)} %get-tuple-element.76, ...), channel_id=1, replica_groups=mesh['dp'=8,'pipe'=4] {'dp','pipe'}, use_global_device_ids=true, to_apply=%region_36.37 | all-reduce | flops 3840 | bytes 30720 | tf_op jit(solution)/shard_map/psum | solution.py:252
  233.4 358.4 %all-reduce.5.cloned.1.call-done = (f32[768,2304]{1,0:T(8,128)}, f32[768,768]{1,0:T(8,128)}, f32[768,3072]{1,0:T(8,128)}, f32[3072,768]{1,0:T(8,128)}) async-done(((f32[768,2304]{1,0:T(8,128)}, f32[768,768]{1,0:T(8,128)}, f32[768,3072]{1,0:T(8,128)}, f32[3072,768]{1,0:T(8,128)}), (f32[768,2304]{1,0:T(8,128)}, f32[768,768]{1,0:T(8,128)}, f32[768,3072]{1,0:T(8,128)}, ...) | async-done | bytes 28311568 | tf_op jit(solution)/shard_map/psum | solution.py:252
  591.8 3.3 constant_dynamic-slice_fusion.1
  595.1 2.8 constant_dynamic-slice_fusion.3
  597.9 1.9 constant_dynamic-slice_fusion.2
  599.8 3.2 constant_dynamic-slice_fusion
  (31 shorter events, 15.7 us)
Async XLA Ops:
  7.2 22.6 %all-gather.2.cloned.1.call-start = ((), (), s32[]{:S(2)}) async-start(), calls=%async_computation.3 | async-start | bytes 1474560 | tf_op jit(solution)/shard_map/all_gather | solution.py:198
  9.6 11.7 %all-to-all-start = ((bf16[4,64,768]{2,1,0:T(8,128)(2,1)}), bf16[4,64,768]{2,1,0:T(8,128)(2,1)S(1)}, u32[]{:S(2)}, u32[]{:S(2)}) async-start(bf16[4,64,768]{2,1,0:T(8,128)(2,1)} %concatenate.21), calls=%async_computation | async-start | bytes 786432 | tf_op jit(solution)/shard_map/all_to_all | solution.py:203
  13.9 578.0 %all-reduce.5.cloned.1.call-start = ((), (), s32[]{:S(2)}) async-start(), calls=%async_computation.4 | async-start | bytes 56623104 | tf_op jit(solution)/shard_map/psum | solution.py:252
  54.8 123.1 %all-to-all-start.1 = ((bf16[4,2,24576]{2,1,0:T(2,128)(2,1)}), bf16[4,2,24576]{2,1,0:T(2,128)(2,1)S(1)}, u32[]{:S(2)}, u32[]{:S(2)}) async-start(bf16[4,2,24576]{2,1,0:T(2,128)(2,1)} %reshape.259), calls=%async_computation.1 | async-start | bytes 786432 | tf_op jit(solution)/shard_map/all_to_all | solution.py:247
  177.9 54.2 %all-to-all-start.2 = ((bf16[4,2,24576]{2,1,0:T(2,128)(2,1)}), bf16[4,2,24576]{2,1,0:T(2,128)(2,1)S(1)}, u32[]{:S(2)}, u32[]{:S(2)}) async-start(bf16[4,2,24576]{2,1,0:T(2,128)(2,1)} %reshape.261), calls=%async_computation.2 | async-start | bytes 786432 | tf_op jit(solution)/shard_map/all_to_all | solution.py:243
Sparse Core Ops, SparseCore 0:
  9.6 20.1 all-gather.1
  48.8 543.0 all-reduce.4
where the time goes:
time: 614 us; the launch traced here: 610 us
  waiting for transfers between devices  378 us (62%)
  starting transfers between devices  119 us (19%)
  blocking collectives  45.8 us (7%)
  local copies, waits for them, and re-layouts  42.6 us (7%)
  between operations  14.2 us (2%)
  other arithmetic  10.5 us (2%)
    psum x1, waiting for transfers between devices, shards(): summed = lax.psum(grad_all, ('dp', 'pipe'))  358 us
    all_to_all x1, starting transfers between devices, shards(): lax.all_to_all(second_out.astype(jnp.bfloat16)[None], 'pipe', split_axis=...  111 us
    psum x1, blocking collectives, shards(): summed = lax.psum(grad_all, ('dp', 'pipe'))  45.8 us
    another operation x11, local copies, waits for them, and re-layouts  18.9 us
    dynamic_slice x9, local copies, waits for them, and re-layouts, shards(): lax.dynamic_slice_in_dim(array, section_index * (array.shape[0] // sectio...  14.4 us
  transfers between devices with their start and end apart: 5, of which 4 were waited for; matrix products, arithmetic and copies ran while one was open for 4% of the time, Pallas kernels for 0%

commit v1 on v0

v1 whole, which is shorter than its diff:
```python
import functools

import jax
import jax.numpy as jnp
from jax import lax
from jax.experimental import pallas as pl
from jax.experimental.pallas import tpu as pltpu
from jax.sharding import PartitionSpec as P

MESH = pl.DeviceIdType.MESH
HEADS = 12
HEAD = 64
F32 = jnp.float32
BF16 = jnp.bfloat16
ANY = pl.BlockSpec(memory_space=pl.ANY)
VMEM = pl.BlockSpec(memory_space=pltpu.VMEM)
SMEM = pl.BlockSpec(memory_space=pltpu.SMEM)


def dot(left, right):
    return jnp.dot(left, right, preferred_element_type=F32)


def dot_nt(left, right):
    return lax.dot_general(left, right, (((1,), (1,)), ((), ())), preferred_element_type=F32)


def normalize(values):
    center = values - jnp.mean(values, axis=-1, keepdims=True)
    scale = lax.rsqrt(jnp.mean(center * center, axis=-1, keepdims=True) + 1e-05)
    return center * scale, scale


def chain_kernel(
    x_ref, cot_ref, len_ref, gain1_ref, shift1_ref, gain2_ref, shift2_ref, embed_ref,
    wqkv_hbm, wout_hbm, wup_hbm, wdown_hbm,
    left_hbm, right_hbm, out_ref, grad_ref, vec_ref,
    wqkv, wout, wup, wdown, left, right, qkv, vt, kt, lse, gp, mixed, state, ctx,
    dk_more, dv_more, dqt, dctx, bias, w_sem, o_sem,
):
    seq, feat = x_ref.shape
    ff = wup.shape[1]
    tiles = ff // feat
    half = feat // 6
    weight_copies = [
        pltpu.make_async_copy(src, dst, w_sem.at[i])
        for i, (src, dst) in enumerate(
            ((wqkv_hbm, wqkv), (wout_hbm, wout), (wup_hbm, wup), (wdown_hbm, wdown))
        )
    ]
    for copy in weight_copies:
        copy.start()

    length = len_ref[0]
    keys = lax.broadcasted_iota(jnp.int32, (seq, seq), 0)
    queries = lax.broadcasted_iota(jnp.int32, (seq, seq), 1)
    bias[...] = jnp.where((keys <= queries) & (keys < length), 0.0, -1e30).astype(F32)
    inside = (lax.broadcasted_iota(jnp.int32, (seq, 1), 0) < length).astype(F32)
    low_lanes = lax.broadcasted_iota(jnp.int32, (seq, half), 1) < HEAD

    def pick(values, head):
        zero = jnp.zeros_like(values)
        return jnp.where(low_lanes, values, zero) if head == 0 else jnp.where(low_lanes, zero, values)

    def rows_of(i):
        return pl.ds(i * seq, seq)

    def put_left(offset, i, values):
        left[pl.ds(offset, values.shape[1]), rows_of(i)] = values.T

    N2, CTX, N1 = ff, ff + feat, ff + 2 * feat
    HID, ATT, QKV = feat, feat + ff, 2 * feat + ff

    def forward(i):
        value = state[i]
        n1 = (normalize(value)[0] * gain1_ref[...] + shift1_ref[...]).astype(BF16)
        put_left(N1, i, n1)
        if i == 0:
            weight_copies[0].wait()
        for j in range(3):
            part = dot(n1, wqkv[:, j * feat : (j + 1) * feat])
            if j == 0:
                part = part * HEAD ** (-0.5)
            part = part.astype(BF16)
            qkv[i, :, j * feat : (j + 1) * feat] = part
            if j == 1:
                kt[i] = part.T
            if j == 2:
                vt[i] = part.T

        def pair(hp, carry):
            lanes = pl.ds(pl.multiple_of(hp * half, half), half)
            q2 = qkv[i, :, lanes]
            for head in range(2):
                qm = pick(q2, head)
                scores = []
                for b in range(i + 1):
                    k2 = qkv[b, :, pl.ds(pl.multiple_of(feat + hp * half, half), half)]
                    scores.append(dot_nt(k2, qm) + bias[...])
                top = jnp.max(scores[0], axis=0, keepdims=True)
                for s in scores[1:]:
                    top = jnp.maximum(top, jnp.max(s, axis=0, keepdims=True))
                weights = [jnp.exp(s - top) for s in scores]
                total = jnp.sum(weights[0], axis=0, keepdims=True)
                for w in weights[1:]:
                    total = total + jnp.sum(w, axis=0, keepdims=True)
                inv = 1.0 / total
                lse[i, pl.ds(2 * hp + head, 1), :] = top + jnp.log(total)
                rows = pl.ds(pl.multiple_of(hp * half + head * HEAD, HEAD), HEAD)
                acc = None
                for b in range(i + 1):
                    term = dot(vt[b, rows, :], (weights[b] * inv).astype(BF16))
                    acc = term if acc is None else acc + term
                left[pl.ds(pl.multiple_of(CTX + hp * half + head * HEAD, HEAD), HEAD), rows_of(i)] = acc.astype(BF16)
            return carry

        lax.fori_loop(0, feat // half, pair, 0)
        ctx[...] = left[pl.ds(CTX, feat), rows_of(i)].T
        if i == 0:
            weight_copies[1].wait()
        mix = state[i] + dot(ctx[...], wout[...])
        mixed[i] = mix
        n2 = (normalize(mix)[0] * gain2_ref[...] + shift2_ref[...]).astype(BF16)
        put_left(N2, i, n2)
        if i == 0:
            weight_copies[2].wait()
            weight_copies[3].wait()
        acc = mix
        for j in range(tiles):
            u = dot(n2, wup[:, j * feat : (j + 1) * feat])
            c = 0.7978845608028654
            square = u * u
            th = jnp.tanh(c * u * (1.0 + 0.044715 * square))
            halfp = 0.5 + 0.5 * th
            active = (u * halfp).astype(BF16)
            slope = halfp + 0.5 * u * (1.0 - th * th) * (c * (1.0 + 3 * 0.044715 * square))
            gp[i, :, j * feat : (j + 1) * feat] = slope.astype(BF16)
            put_left(j * feat, i, active)
            acc = acc + dot(active, wdown[j * feat : (j + 1) * feat, :])
        return acc

    def norm_back(values, d_out, gain, slot, first):
        norm, scale = normalize(values)
        g_gain = jnp.sum(d_out * norm, axis=0, keepdims=True)
        g_shift = jnp.sum(d_out, axis=0, keepdims=True)
        if first:
            vec_ref[slot : slot + 1, :] = g_gain
            vec_ref[slot + 1 : slot + 2, :] = g_shift
        else:
            vec_ref[slot : slot + 1, :] += g_gain
            vec_ref[slot + 1 : slot + 2, :] += g_shift
        t = d_out * gain
        return scale * (t - jnp.mean(t, axis=-1, keepdims=True) - norm * jnp.mean(t * norm, axis=-1, keepdims=True))

    def backward(i, grad):
        branch = grad.astype(BF16)
        right[rows_of(i), 0:feat] = branch
        acc = None
        for j in range(tiles):
            d_active = dot_nt(branch, wdown[j * feat : (j + 1) * feat, :])
            d_hidden = (d_active * gp[i, :, j * feat : (j + 1) * feat].astype(F32)).astype(BF16)
            right[rows_of(i), HID + j * feat : HID + (j + 1) * feat] = d_hidden
            term = dot_nt(d_hidden, wup[:, j * feat : (j + 1) * feat])
            acc = term if acc is None else acc + term
        d_mixed = grad + norm_back(mixed[i], acc, gain2_ref[...], 2, i == 1)
        d_attn = d_mixed.astype(BF16)
        right[rows_of(i), ATT : ATT + feat] = d_attn
        dctx[...] = dot_nt(d_attn, wout[...]).astype(BF16)

        def pair(hp, carry):
            lanes = pl.ds(pl.multiple_of(hp * half, half), half)
            q2 = qkv[i, :, lanes]
            do2 = dctx[:, lanes]
            dk = [None] * (i + 1)
            dv = [None] * (i + 1)
            for head in range(2):
                qm = pick(q2, head)
                dom = pick(do2, head)
                row = lse[i, pl.ds(2 * hp + head, 1), :]
                soft, d_soft = [], []
                inner = None
                for b in range(i + 1):
                    k2 = qkv[b, :, pl.ds(pl.multiple_of(feat + hp * half, half), half)]
                    v2 = qkv[b, :, pl.ds(pl.multiple_of(2 * feat + hp * half, half), half)]
                    soft.append(jnp.exp(dot_nt(k2, qm) + (bias[...] - row)))
                    d_soft.append(dot_nt(v2, dom))
                    term = jnp.sum(soft[b] * d_soft[b], axis=0, keepdims=True)
                    inner = term if inner is None else inner + term
                rows = pl.ds(pl.multiple_of(hp * half + head * HEAD, HEAD), HEAD)
                dq = None
                for b in range(i + 1):
                    d_score = (soft[b] * (d_soft[b] - inner)).astype(BF16)
                    term_v = dot(soft[b].astype(BF16), dom)
                    term_k = dot(d_score, qm)
                    term_q = dot(kt[b, rows, :], d_score)
                    dv[b] = term_v if dv[b] is None else dv[b] + term_v
                    dk[b] = term_k if dk[b] is None else dk[b] + term_k
                    dq = term_q if dq is None else dq + term_q
                dqt[rows, :] = (dq * HEAD ** (-0.5)).astype(BF16)
            dk_own, dv_own = dk[i], dv[i]
            if i == 1:
                dk_more[:, lanes] = dk[0]
                dv_more[:, lanes] = dv[0]
            else:
                dk_own = dk_own + dk_more[:, lanes]
                dv_own = dv_own + dv_more[:, lanes]
            right[rows_of(i), pl.ds(pl.multiple_of(QKV + feat + hp * half, half), half)] = dk_own.astype(BF16)
            right[rows_of(i), pl.ds(pl.multiple_of(QKV + 2 * feat + hp * half, half), half)] = dv_own.astype(BF16)
            return carry

        lax.fori_loop(0, feat // half, pair, 0)
        right[rows_of(i), QKV : QKV + feat] = dqt[...].T
        d_normed = None
        for j in range(3):
            term = dot_nt(
                right[rows_of(i), QKV + j * feat : QKV + (j + 1) * feat], wqkv[:, j * feat : (j + 1) * feat]
            )
            d_normed = term if d_normed is None else d_normed + term
        return d_mixed + norm_back(state[i], d_normed, gain1_ref[...], 0, i == 1)

    state[0] = x_ref[...].astype(F32)
    first = forward(0)
    state[1] = first.astype(BF16).astype(F32) + embed_ref[...]
    second = forward(1)
    out_ref[...] = (second * inside).astype(BF16)
    left_copy = pltpu.make_async_copy(left, left_hbm, o_sem.at[0])
    left_copy.start()
    d_carry = backward(1, cot_ref[...].astype(F32) * inside)
    vec_ref[4:5, :] = jnp.sum(d_carry, axis=0, keepdims=True)
    vec_ref[5:8, :] = jnp.zeros((3, feat), F32)
    d_state = backward(0, d_carry.astype(BF16).astype(F32))
    grad_ref[...] = d_state.astype(BF16)
    right_copy = pltpu.make_async_copy(right, right_hbm, o_sem.at[1])
    right_copy.start()
    left_copy.wait()
    right_copy.wait()


def run_chain(x, cot, length, gain1, shift1, gain2, shift2, embed, w_qkv, w_out, w_up, w_down):
    seq, feat = x.shape
    ff = w_up.shape[1]
    rows = [v.reshape(1, feat) for v in (gain1, shift1, gain2, shift2, embed)]
    left_rows = ff + 3 * feat
    right_cols = 5 * feat + ff
    return pl.pallas_call(
        chain_kernel,
        out_shape=(
            jax.ShapeDtypeStruct((left_rows, 2 * seq), BF16),
            jax.ShapeDtypeStruct((2 * seq, right_cols), BF16),
            jax.ShapeDtypeStruct((seq, feat), BF16),
            jax.ShapeDtypeStruct((seq, feat), BF16),
            jax.ShapeDtypeStruct((8, feat), F32),
        ),
        in_specs=[VMEM, VMEM, SMEM] + [VMEM] * 5 + [ANY] * 4,
        out_specs=(ANY, ANY, VMEM, VMEM, VMEM),
        scratch_shapes=[
            pltpu.VMEM(w_qkv.shape, BF16),
            pltpu.VMEM(w_out.shape, BF16),
            pltpu.VMEM(w_up.shape, BF16),
            pltpu.VMEM(w_down.shape, BF16),
            pltpu.VMEM((left_rows, 2 * seq), BF16),
            pltpu.VMEM((2 * seq, right_cols), BF16),
            pltpu.VMEM((2, seq, 3 * feat), BF16),
            pltpu.VMEM((2, feat, seq), BF16),
            pltpu.VMEM((2, feat, seq), BF16),
            pltpu.VMEM((2, 16, seq), F32),
            pltpu.VMEM((2, seq, ff), BF16),
            pltpu.VMEM((2, seq, feat), F32),
            pltpu.VMEM((2, seq, feat), F32),
            pltpu.VMEM((seq, feat), BF16),
            pltpu.VMEM((seq, feat), F32),
            pltpu.VMEM((seq, feat), F32),
            pltpu.VMEM((feat, seq), BF16),
            pltpu.VMEM((seq, feat), BF16),
            pltpu.VMEM((seq, seq), F32),
            pltpu.SemaphoreType.DMA((4,)),
            pltpu.SemaphoreType.DMA((2,)),
        ],
        compiler_params=pltpu.CompilerParams(vmem_limit_bytes=58 * 2**20),
    )(x, cot, length, *rows, w_qkv, w_out, w_up, w_down)


def exchange_kernel(in_ref, cot_ref, x_ref, c_ref, x_send, x_recv, c_send, c_recv, local):
    g = lax.axis_index("dp")
    p = lax.axis_index("pipe")
    slots, block, feat = in_ref.shape
    size = slots + 1
    barrier = pltpu.get_barrier_semaphore()
    for j in range(1, size):
        pl.semaphore_signal(barrier, inc=1, device_id=(g, (p + j) % size), device_id_type=MESH)
    pl.semaphore_wait(barrier, size - 1)
    mine = pl.ds(pl.multiple_of(p * block, block), block)

    def copies(j):
        peer = (p + j) % size
        slot = jnp.maximum(peer - 1, 0)
        return [
            pltpu.make_async_remote_copy(
                src.at[slot], dst.at[mine], send.at[j - 1], recv.at[j - 1],
                device_id=(g, peer), device_id_type=MESH,
            )
            for src, dst, send, recv in ((in_ref, x_ref, x_send, x_recv), (cot_ref, c_ref, c_send, c_recv))
        ]

    for j in range(1, size):
        @pl.when((p + j) % size > 0)
        def _(j=j):
            for copy in copies(j):
                copy.start()

    @pl.when(p > 0)
    def _():
        own = [
            pltpu.make_async_copy(in_ref.at[p - 1], x_ref.at[mine], local.at[0]),
            pltpu.make_async_copy(cot_ref.at[p - 1], c_ref.at[mine], local.at[1]),
        ]
        for copy in own:
            copy.start()
        for copy in own:
            copy.wait()
        for j in range(1, size):
            for copy in copies(j):
                copy.wait_recv()

    @pl.when(p == 0)
    def _():
        x_ref[...] = jnp.zeros(x_ref.shape, x_ref.dtype)
        c_ref[...] = jnp.zeros(c_ref.shape, c_ref.dtype)

    for j in range(1, size):
        @pl.when((p + j) % size > 0)
        def _(j=j):
            for copy in copies(j):
                copy.wait_send()


def run_exchange(inputs, cotangent):
    slots, block, feat = inputs.shape
    size = slots + 1
    whole = jax.ShapeDtypeStruct((size * block, feat), BF16)
    return pl.pallas_call(
        exchange_kernel,
        out_shape=(whole, whole),
        in_specs=[VMEM, VMEM],
        out_specs=(VMEM, VMEM),
        scratch_shapes=[pltpu.SemaphoreType.DMA((size - 1,))] * 4 + [pltpu.SemaphoreType.DMA((2,))],
        compiler_params=pltpu.CompilerParams(collective_id=0, has_side_effects=True),
    )(inputs, cotangent)


ZED = 4


def reduce_kernel(
    dims, left_hbm, right_hbm, out_seq, grad_seq, vec_in,
    sums_hbm, out_ref, gin_ref, vec_ref,
    left, right, own, give, d_recv, y_send, y_keep, y_recv, x_send, x_keep, x_recv,
    z_send, z_recv, w_send, w_recv, full, vec_recv,
    l_sem, r_sem, d_ss, d_rs, y_ss, y_rs, x_ss, x_rs, z_ss, z_rs, w_ss, w_rs, g_ss, g_rs, h_ss, h_rs, s_sem,
    o_ss, o_rs, v_ss, v_rs, local,
):
    feat, ff, rows, lags, groups = dims
    units = (2 * ff + 4 * feat) // feat
    quarter = feat // 4
    subs = quarter // rows
    chunks = units * subs
    tiles = ff // feat
    piece = rows // ZED
    g = lax.axis_index("dp")
    p = lax.axis_index("pipe")
    core, y = p % 2, p // 2
    x, z, w = g % 2, (g // 2) % ZED, g // (2 * ZED)
    sib = (g, p + 1 - 2 * core)
    ypeer = (g, p + 2 - 4 * y)
    diag = (g, 3 - p)
    xpeer = (g + 1 - 2 * x, p)

    def zpeer(j):
        return (g + 2 * ((z + j) % ZED - z), p)

    def wpeer(j):
        return (g + 2 * ZED * ((w + j) % groups - w), p)

    everyone = [sib, ypeer, diag, xpeer] + [zpeer(j) for j in range(1, ZED)] + [wpeer(j) for j in range(1, groups)]

    loads_r = [
        pltpu.make_async_copy(
            right_hbm.at[:, pl.ds(u * feat, feat)], right.at[:, pl.ds(u * feat, feat)], r_sem.at[u]
        )
        for u in range(units - tiles + 1)
    ]
    starts = (0, ff, ff + feat, ff + 2 * feat, ff + 3 * feat)
    loads_l = [
        pltpu.make_async_copy(left_hbm.at[pl.ds(a, b - a)], left.at[pl.ds(a, b - a)], l_sem.at[i])
        for i, (a, b) in enumerate(zip(starts[:-1], starts[1:]))
    ]
    loads_r[0].start()
    loads_l[0].start()
    loads_l[1].start()
    for copy in loads_r[1:]:
        copy.start()
    loads_l[2].start()
    loads_l[3].start()

    barrier = pltpu.get_barrier_semaphore()
    for device in everyone:
        pl.semaphore_signal(barrier, inc=1, device_id=device, device_id_type=MESH)
    pl.semaphore_wait(barrier, len(everyone))

    slots, block, _ = out_ref.shape
    size = slots + 1

    def result_copies(j):
        peer = (p + j) % size
        slot = jnp.maximum(p - 1, 0)
        part = pl.ds(pl.multiple_of(peer * block, block), block)
        return [
            pltpu.make_async_remote_copy(
                src.at[part], dst.at[slot], o_ss.at[n, j - 1], o_rs.at[n, j - 1],
                device_id=(g, peer), device_id_type=MESH,
            )
            for n, (src, dst) in enumerate(((out_seq, out_ref), (grad_seq, gin_ref)))
        ]

    def own_results():
        part = pl.ds(pl.multiple_of(p * block, block), block)
        slot = jnp.maximum(p - 1, 0)
        return [
            pltpu.make_async_copy(out_seq.at[part], out_ref.at[slot], local.at[0]),
            pltpu.make_async_copy(grad_seq.at[part], gin_ref.at[slot], local.at[1]),
        ]

    def copy_d(c):
        return pltpu.make_async_remote_copy(
            give.at[c % 2], d_recv.at[c], d_ss.at[c], d_rs.at[c], device_id=sib, device_id_type=MESH
        )

    def copy_y(c):
        return pltpu.make_async_remote_copy(
            y_send.at[c], y_recv.at[c], y_ss.at[c], y_rs.at[c], device_id=ypeer, device_id_type=MESH
        )

    def copy_x(c):
        return pltpu.make_async_remote_copy(
            x_send.at[c], x_recv.at[c], x_ss.at[c], x_rs.at[c], device_id=xpeer, device_id_type=MESH
        )

    def part_of(k):
        return pl.ds(pl.multiple_of(k * piece, piece), piece)

    def copy_z(c, j):
        return pltpu.make_async_remote_copy(
            z_send.at[c, part_of((z + j) % ZED)], z_recv.at[c, j - 1], z_ss.at[c, j - 1], z_rs.at[c, j - 1],
            device_id=zpeer(j), device_id_type=MESH,
        )

    def copy_w(c, j):
        return pltpu.make_async_remote_copy(
            w_send.at[c], w_recv.at[c, j - 1], w_ss.at[c, j - 1], w_rs.at[c, j - 1],
            device_id=wpeer(j), device_id_type=MESH,
        )

    def copy_g(c, j):
        place = full.at[c, x, part_of(z)]
        return pltpu.make_async_remote_copy(
            place, place, g_ss.at[c, j - 1], g_rs.at[c, j - 1], device_id=zpeer(j), device_id_type=MESH
        )

    def copy_h(c):
        place = full.at[c, x]
        return pltpu.make_async_remote_copy(
            place, place, h_ss.at[c], h_rs.at[c], device_id=xpeer, device_id_type=MESH
        )

    def copy_s(c):
        u, s = c // subs, c % subs
        half = feat // 2
        return [
            pltpu.make_async_copy(
                full.at[c, h],
                sums_hbm.at[
                    pl.ds(pl.multiple_of(s * rows, rows), rows),
                    pl.ds(pl.multiple_of(u * feat + h * half, half), half),
                ],
                s_sem.at[c, h],
            )
            for h in range(2)
        ]

    def make(c):
        u, s = c // subs, c % subs

        def left_rows(q):
            down = feat * q + quarter * u
            rest = ff + feat * ((u >= 2 * tiles).astype(jnp.int32) + (u > 2 * tiles).astype(jnp.int32)) + quarter * q
            start = jnp.where(u < tiles, down, rest) + s * rows
            return left[pl.ds(pl.multiple_of(start, rows), rows), :]

        order = (2 * (1 - y) + core, 2 * y + core, 2 * (1 - y) + 1 - core, 2 * y + 1 - core)
        lhs = jnp.concatenate([left_rows(q) for q in order], axis=0)
        cols = pl.ds(pl.multiple_of(feat * jnp.maximum(u - tiles + 1, 0), feat), feat)
        total = jnp.dot(lhs, right[:, cols], preferred_element_type=F32)
        slot = c % 2
        own[slot, 0] = total[:rows]
        own[slot, 1] = total[rows : 2 * rows]
        give[slot, 0] = total[2 * rows : 3 * rows].astype(BF16)
        give[slot, 1] = total[3 * rows :].astype(BF16)
        copy_d(c).start()

    def stage_y(c):
        copy_d(c).wait()
        slot = c % 2
        y_send[c] = (own[slot, 0] + d_recv[c, 0].astype(F32)).astype(BF16)
        copy_y(c).start()
        y_keep[c % 4] = own[slot, 1] + d_recv[c, 1].astype(F32)

    def stage_x(c):
        copy_y(c).wait()
        half = feat // 2
        total = y_keep[c % 4] + y_recv[c].astype(F32)

        @pl.when(x == 0)
        def _():
            x_send[c] = total[:, half:].astype(BF16)
            x_keep[c % 4] = total[:, :half]

        @pl.when(x == 1)
        def _():
            x_send[c] = total[:, :half].astype(BF16)
            x_keep[c % 4] = total[:, half:]

        copy_x(c).start()

    def stage_z(c):
        copy_x(c).wait()
        total = x_keep[c % 4] + x_recv[c].astype(F32)
        z_send[c] = total.astype(BF16)
        for j in range(1, ZED):
            copy_z(c, j).start()

    def add_z(c):
        for j in range(1, ZED):
            copy_z(c, j).wait()
        total = z_send[c, part_of(z)].astype(F32)
        for j in range(1, ZED):
            total = total + z_recv[c, j - 1].astype(F32)
        return total

    def stage_w(c):
        w_send[c] = add_z(c).astype(BF16)
        for j in range(1, groups):
            copy_w(c, j).start()

    def add_w(c):
        for j in range(1, groups):
            copy_w(c, j).wait()
        total = w_send[c].astype(F32)
        for j in range(1, groups):
            total = total + w_recv[c, j - 1].astype(F32)
        return total

    def stage_g(c):
        full[c, x, part_of(z)] = (add_z(c) if groups == 1 else add_w(c)).astype(BF16)
        for j in range(1, ZED):
            copy_g(c, j).start()

    def stage_h(c):
        for j in range(1, ZED):
            copy_g(c, j).wait()
        copy_h(c).start()

    def stage_s(c):
        copy_h(c).wait()
        for copy in copy_s(c):
            copy.start()

    ways = [[sib], [ypeer], [xpeer], [zpeer(j) for j in range(1, ZED)]]
    if groups > 1:
        ways.append([wpeer(j) for j in range(1, groups)])
    firsts = [sum(len(way) for way in ways[:i]) for i in range(len(ways))]

    def vector_copies(i):
        return [
            pltpu.make_async_remote_copy(
                vec_ref.at[i], vec_recv.at[firsts[i] + n], v_ss.at[firsts[i] + n], v_rs.at[firsts[i] + n],
                device_id=device, device_id_type=MESH,
            )
            for n, device in enumerate(ways[i])
        ]

    def vector_step(i):
        if i == 0:
            vec_ref[0] = vec_in[...]
        else:
            for copy in vector_copies(i - 1):
                copy.wait()
            total = vec_ref[i - 1]
            for n in range(len(ways[i - 1])):
                total = total + vec_recv[firsts[i - 1] + n]
            vec_ref[i] = total
        if i < len(ways):
            for copy in vector_copies(i):
                copy.start()

    stages = [make, stage_y, stage_x, stage_z] + ([stage_w] if groups > 1 else []) + [stage_g, stage_h, stage_s]
    offsets = [sum(lags[: i + 1]) for i in range(len(stages))]

    def step(t, carry):
        u, s = t // subs, t % subs
        for k in range(len(loads_r)):
            first = 0 if k == 0 else (tiles - 1 + k) * subs

            @pl.when(t == first)
            def _(k=k):
                loads_r[k].wait()

        for k, first in enumerate((0, tiles * subs, 2 * tiles * subs, (2 * tiles + 1) * subs)):
            @pl.when(t == first)
            def _(k=k):
                loads_l[k].wait()

        for stage, offset in zip(stages, offsets):
            c = t - offset

            @pl.when((c >= 0) & (c < chunks))
            def _(stage=stage, c=c):
                stage(c)

        for i in range(len(ways) + 1):
            @pl.when(t == 2 + 3 * i)
            def _(i=i):
                vector_step(i)

        @pl.when(t == 1)
        def _():
            @pl.when(p > 0)
            def _():
                for j in range(1, size):
                    for copy in result_copies(j):
                        copy.start()
                for copy in own_results():
                    copy.start()

        return carry

    lax.fori_loop(0, chunks + offsets[-1], step, 0)

    @pl.when(p > 0)
    def _():
        for copy in own_results():
            copy.wait()
        for j in range(1, size):
            for copy in result_copies(j):
                copy.wait_send()

    for j in range(1, size):
        source = (p + size - j) % size

        @pl.when(source > 0)
        def _(j=j, source=source):
            for n, dst in enumerate((out_ref, gin_ref)):
                pltpu.make_async_copy(dst.at[source - 1], dst.at[source - 1], o_rs.at[n, j - 1]).wait()

    def finish(c, carry):
        for copy in copy_s(c):
            copy.wait()
        return carry

    lax.fori_loop(0, chunks, finish, 0)


def run_reduce(rows, lags, groups, left, right, out_seq, grad_seq, vec, slots):
    seq, feat = out_seq.shape
    ff = left.shape[0] - 3 * feat
    quarter = feat // 4
    units = (2 * ff + 4 * feat) // feat
    chunks = units * (quarter // rows)
    piece = rows // ZED
    half = feat // 2
    steps = 4 + (groups > 1)
    landings = 6 + (groups - 1)
    more = max(groups - 1, 1)
    dma = pltpu.SemaphoreType.DMA
    block = seq // (slots + 1)
    local_block = jax.ShapeDtypeStruct((slots, block, feat), BF16)
    return pl.pallas_call(
        functools.partial(reduce_kernel, (feat, ff, rows, lags, groups)),
        out_shape=(
            jax.ShapeDtypeStruct((quarter, units * feat), BF16),
            local_block,
            local_block,
            jax.ShapeDtypeStruct((steps + 1, 8, feat), F32),
        ),
        in_specs=[ANY, ANY, VMEM, VMEM, VMEM],
        out_specs=(ANY, VMEM, VMEM, VMEM),
        scratch_shapes=[
            pltpu.VMEM(left.shape, BF16),
            pltpu.VMEM(right.shape, BF16),
            pltpu.VMEM((2, 2, rows, feat), F32),
            pltpu.VMEM((2, 2, rows, feat), BF16),
            pltpu.VMEM((chunks, 2, rows, feat), BF16),
            pltpu.VMEM((chunks, rows, feat), BF16),
            pltpu.VMEM((4, rows, feat), F32),
            pltpu.VMEM((chunks, rows, feat), BF16),
            pltpu.VMEM((chunks, rows, half), BF16),
            pltpu.VMEM((4, rows, half), F32),
            pltpu.VMEM((chunks, rows, half), BF16),
            pltpu.VMEM((chunks, rows, half), BF16),
            pltpu.VMEM((chunks, ZED - 1, piece, half), BF16),
            pltpu.VMEM((chunks if groups > 1 else 1, piece, half), BF16),
            pltpu.VMEM((chunks if groups > 1 else 1, more, piece, half), BF16),
            pltpu.VMEM((chunks, 2, rows, half), BF16),
            pltpu.VMEM((landings, 8, feat), F32),
            dma((4,)), dma((units,)),
            dma((chunks,)), dma((chunks,)), dma((chunks,)), dma((chunks,)), dma((chunks,)), dma((chunks,)),
            dma((chunks, ZED - 1)), dma((chunks, ZED - 1)),
            dma((chunks, more)), dma((chunks, more)),
            dma((chunks, ZED - 1)), dma((chunks, ZED - 1)),
            dma((chunks,)), dma((chunks,)), dma((chunks, 2)),
            dma((2, slots)), dma((2, slots)), dma((landings,)), dma((landings,)), dma((2,)),
        ],
        compiler_params=pltpu.CompilerParams(
            collective_id=1, has_side_effects=True, vmem_limit_bytes=58 * 2**20
        ),
    )(left, right, out_seq, grad_seq, vec)


def shards(
    inputs, lengths, w_qkv, w_out, w_up, w_down, norm1_gain, norm1_shift, norm2_gain, norm2_shift, pass_embed, cotangent
):
    p = lax.axis_index("pipe")
    slots, block, feat = inputs.shape
    ff = w_up.shape[1]
    groups = lax.axis_size("dp") // (2 * ZED)
    x, cot = run_exchange(inputs, cotangent)
    length = lax.dynamic_slice_in_dim(lengths, jnp.maximum(p - 1, 0), 1, 0)
    left, right, out_seq, grad_seq, vec = run_chain(
        x, cot, length, norm1_gain, norm1_shift, norm2_gain, norm2_shift, pass_embed, w_qkv, w_out, w_up, w_down
    )
    sums, block_out, input_grads, vecs = run_reduce(
        ROWS, LAGS[: 7 + (groups > 1)], groups, left, right, out_seq, grad_seq, vec, slots
    )
    quarter = feat // 4
    tiles = ff // feat
    down = jnp.concatenate([sums[:, j * feat : (j + 1) * feat] for j in range(tiles)], axis=0).astype(F32)
    up = sums[:, ff : 2 * ff].astype(F32)
    out = sums[:, 2 * ff : 2 * ff + feat].astype(F32)
    qkv = sums[:, 2 * ff + feat :].astype(F32)
    vector = lax.dynamic_slice_in_dim(vecs[-1], p * quarter, quarter, 1)
    return (block_out, input_grads, qkv, out, up, down) + tuple(vector[i] for i in range(5))


ROWS = 64
LAGS = (0, 1, 3, 2, 3, 3, 2, 2)


def solution(mesh):
    rep = P()
    seqs = P("dp", "pipe", None)
    return jax.shard_map(
        shards,
        mesh=mesh,
        in_specs=(seqs, P("dp")) + (rep,) * 9 + (seqs,),
        out_specs=(seqs, seqs) + (P("pipe", None),) * 4 + (P("pipe"),) * 5,
        check_vma=False,
    )
```

time: 614 us -> 209 us (0.34)
  waiting for transfers between devices: 378 us -> 0 us
  Pallas kernels: 0 us -> 188 us
  starting transfers between devices: 119 us -> 0 us
  blocking collectives: 45.8 us -> 0 us
  local copies, waits for them, and re-layouts: 42.6 us -> 12.2 us
  between operations: 14.2 us -> 0.68 us
    psum x1 -> x0, waiting for transfers between devices: 358 us -> none  [shards(): summed = lax.psum(grad_all, ('dp', 'pipe'))]
    pallas_call x0 -> x3, Pallas kernels: none -> 188 us  [the longest x1 123 us: run_reduce(): pl.pallas_call(functools.partial(reduce_kernel, (feat, ff, rows, lags, gr...]
    all_to_all x3 -> x0, starting transfers between devices: 119 us -> none  [the longest x1 111 us: shards(): lax.all_to_all(second_out.astype(jnp.bfloat16)[None], 'pipe', split_axis=...]
    psum x1 -> x0, blocking collectives: 45.8 us -> none  [shards(): summed = lax.psum(grad_all, ('dp', 'pipe'))]
    another operation x11 -> x0, local copies, waits for them, and re-layouts: 18.9 us -> none
    dynamic_slice x10 -> x1, local copies, waits for them, and re-layouts: 15.6 us -> 1.24 us  [shards(): length = lax.dynamic_slice_in_dim(lengths, jnp.maximum(p - 1, 0), 1, 0)]
    all_to_all x3 -> x0, waiting for transfers between devices: 10.6 us -> none  [the longest x1 6.7 us: shards(): lax.all_to_all(second_out.astype(jnp.bfloat16)[None], 'pipe', split_axis=...]
    all_gather x1 -> x0, waiting for transfers between devices: 8.44 us -> none  [shards(): gathered = lax.all_gather(inputs, 'pipe', axis=1, tiled=True)]
  transfers between devices with their start and end apart: 5 -> 0, of which waited for: 4 -> 0; matrix products, arithmetic and copies ran while one was open for 4% -> 0% of each run, Pallas kernels for 0% -> 0%
where the time goes in v1:
time: 209 us; the launch traced here: 208 us
  Pallas kernels  188 us (90%)
  local copies, waits for them, and re-layouts  12.2 us (6%)
  other arithmetic  6.82 us (3%)
    pallas_call x1, Pallas kernels, run_reduce(): pl.pallas_call(functools.partial(reduce_kernel, (feat, ff, rows, lags, gr...  123 us
    pallas_call x1, Pallas kernels, run_chain(): pl.pallas_call(chain_kernel, out_shape=(jax.ShapeDtypeStruct((left_rows,...  50.9 us
    pallas_call x1, Pallas kernels, run_exchange(): pl.pallas_call(exchange_kernel, out_shape=(whole, whole), in_specs=[VMEM,...  14.1 us
    reshape x5, local copies, waits for them, and re-layouts, run_chain(): rows = [v.reshape(1, feat) for v in (gain1, shift1, gain2, shift2, embed)]  6.34 us

profile of v1, /device:TPU:0, one launch (start us, length us, event | category | flops | bytes accessed | tf_op | source)
XLA Modules:
  0.0 208.1 jit_solution(12254707611347780646)
XLA Ops:
  0.6 14.1 %shard_map.203 = (bf16[256,768]{1,0:T(8,128)(2,1)}, bf16[256,768]{1,0:T(8,128)(2,1)}) custom-call(bf16[3,64,768]{2,1,0:T(8,128)(2,1)} %in_ref.1, bf16[3,64,768]{2,1,0:T(8,128)(2,1)} %cot_ref.1), custom_call_target="tpu_custom_call" | custom-call | tf_op jit(solution)/shard_map/pallas_call | solution.py:341
  14.7 1.2 dynamic_slice.6.len_ref
  16.0 1.3 reshape.48.gain1_ref
  17.2 1.3 reshape.49.shift1_ref
  18.5 1.3 reshape.50.gain2_ref
  19.8 1.3 reshape.51.shift2_ref
  21.1 1.3 reshape.52.embed_ref
  22.3 50.9 %shard_map.204 = (bf16[5376,512]{1,0:T(8,128)(2,1)}, bf16[512,6912]{1,0:T(8,128)(2,1)}, bf16[256,768]{1,0:T(8,128)(2,1)}, bf16[256,768]{1,0:T(8,128)(2,1)}, f32[8,768]{1,0:T(8,128)}) custom-call(bf16[256,768]{1,0:T(8,128)(2,1)} %get-tuple-element.22.x_ref, bf16[256,768]{1,0:T(8,128)(2,1)} %get-tuple-element.23.cot_ref, s32[1]{0:T(128)} %dynamic_slice.6.len_ref, ...), custom_call_target="tpu_custom_call" | custom-call | tf_op jit(solution)/shard_map/pallas_call | solution.py:245
  73.2 123.4 %shard_map.205 = (bf16[192,9216]{1,0:T(8,128)(2,1)}, bf16[3,64,768]{2,1,0:T(8,128)(2,1)}, bf16[3,64,768]{2,1,0:T(8,128)(2,1)}, f32[5,8,768]{2,1,0:T(8,128)}) custom-call(bf16[5376,512]{1,0:T(8,128)(2,1)} %get-tuple-element.24.left_hbm, bf16[512,6912]{1,0:T(8,128)(2,1)} %get-tuple-element.25.right_hbm, bf16[256,768]{1,0:T(8,128)(2,1)} %get-tuple-element.26.out_seq, ...), custom_call_target="tpu_custom_call" | custom-call | tf_op jit(solution)/shard_map/pallas_call | solution.py:686
  196.6 2.3 %fusion = (bf16[192,768]{1,0:T(8,128)(2,1)S(1)}, bf16[192,768]{1,0:T(8,128)(2,1)S(1)}, bf16[192,768]{1,0:T(8,128)(2,1)S(1)}, bf16[192,768]{1,0:T(8,128)(2,1)S(1)}, f32[192,768]{1,0:T(8,128)}) fusion(bf16[192,9216]{1,0:T(8,128)(2,1)} %get-tuple-element.31), kind=kLoop, calls=%fused_computation.9 | loop fusion | flops 147456 | bytes 3244032 | tf_op jit(solution)/shard_map/slice | solution.py:745
  198.9 0.0 copy-start
  198.9 1.6 maximum_convert_fusion
  200.5 1.7 slice.51
  202.2 1.5 constant_dynamic-slice_fusion.4
  203.7 0.0 copy-done
  203.7 0.0 copy-start.2
  203.7 1.7 slice_convert_fusion
  205.4 0.0 copy-start.1
  205.4 1.3 slice_convert_fusion.1
  206.7 0.0 copy-done.2
  206.7 0.7 copy.25
  207.4 0.0 copy-done.1
  207.4 0.7 copy.26
Async XLA Ops:
  198.9 4.8 %copy-start = (bf16[192,9216]{1,0:T(8,128)(2,1)S(1)}, bf16[192,9216]{1,0:T(8,128)(2,1)}, u32[]{:S(2)}) copy-start(bf16[192,9216]{1,0:T(8,128)(2,1)} %get-tuple-element.31) | copy-start | bytes 10616836
  203.7 3.0 %copy-start.2 = (bf16[3,64,768]{2,1,0:T(8,128)(2,1)S(1)}, bf16[3,64,768]{2,1,0:T(8,128)(2,1)}, u32[]{:S(2)}) copy-start(bf16[3,64,768]{2,1,0:T(8,128)(2,1)} %get-tuple-element.54) | copy-start | bytes 884740
  205.4 2.0 copy-start.1

commit v2 on v1

v2 whole, which is shorter than its diff:
```python
import functools

import jax
import jax.numpy as jnp
from jax import lax
from jax.experimental import pallas as pl
from jax.experimental.pallas import tpu as pltpu
from jax.sharding import PartitionSpec as P

MESH = pl.DeviceIdType.MESH
HEADS = 12
HEAD = 64
F32 = jnp.float32
BF16 = jnp.bfloat16
ANY = pl.BlockSpec(memory_space=pl.ANY)
VMEM = pl.BlockSpec(memory_space=pltpu.VMEM)
SMEM = pl.BlockSpec(memory_space=pltpu.SMEM)


def dot(left, right):
    return jnp.dot(left, right, preferred_element_type=F32)


def dot_nt(left, right):
    return lax.dot_general(left, right, (((1,), (1,)), ((), ())), preferred_element_type=F32)


def normalize(values):
    center = values - jnp.mean(values, axis=-1, keepdims=True)
    scale = lax.rsqrt(jnp.mean(center * center, axis=-1, keepdims=True) + 1e-05)
    return center * scale, scale


ZED = 4
SLOTS = 8
ROWS = 64
LAGS = (0, 1, 3, 2, 3, 3, 2, 2)
EARLY = (2, 4)


def block_kernel(
    dims, in_hbm, cot_hbm, len_ref, gain1_ref, shift1_ref, gain2_ref, shift2_ref, embed_ref,
    wqkv_hbm, wout_hbm, wup_hbm, wdown_hbm,
    sums_hbm, out_ref, gin_ref, vec_ref,
    x_ref, cot_ref, out_seq, grad_seq, vec_part, vec_sum,
    wqkv, wout, wup, wdown, left, right, qkv, vt, kt, lse, gp, mixed, state, ctx,
    dk_more, dv_more, dqt, dctx, bias,
    own, give, d_recv, y_send, y_keep, y_recv, x_send, x_keep, x_recv,
    z_send, z_recv, w_send, w_recv, full, vec_recv,
    w_sem, i_ss, i_rs, d_ss, d_rs, y_ss, y_rs, x_ss, x_rs, z_ss, z_rs, w_ss, w_rs, g_ss, g_rs, h_ss, h_rs, s_sem,
    o_ss, o_rs, v_ss, v_rs, local,
):
    rows, lags, groups = dims
    slots, block, feat = in_hbm.shape
    size = slots + 1
    seq = size * block
    ff = wup.shape[1]
    tiles = ff // feat
    half = feat // 6
    units = (2 * ff + 4 * feat) // feat
    quarter = feat // 4
    subs = quarter // rows
    chunks = units * subs
    piece = rows // ZED
    g = lax.axis_index("dp")
    p = lax.axis_index("pipe")
    core, y = p % 2, p // 2
    x, z, w = g % 2, (g // 2) % ZED, g // (2 * ZED)
    sib = (g, p + 1 - 2 * core)
    ypeer = (g, p + 2 - 4 * y)
    diag = (g, 3 - p)
    xpeer = (g + 1 - 2 * x, p)

    def zpeer(j):
        return (g + 2 * ((z + j) % ZED - z), p)

    def wpeer(j):
        return (g + 2 * ZED * ((w + j) % groups - w), p)

    everyone = [sib, ypeer, diag, xpeer] + [zpeer(j) for j in range(1, ZED)] + [wpeer(j) for j in range(1, groups)]

    weight_copies = [
        pltpu.make_async_copy(src, dst, w_sem.at[i])
        for i, (src, dst) in enumerate(
            ((wqkv_hbm, wqkv), (wout_hbm, wout), (wup_hbm, wup), (wdown_hbm, wdown))
        )
    ]
    for copy in weight_copies:
        copy.start()

    barrier = pltpu.get_barrier_semaphore()
    for device in everyone:
        pl.semaphore_signal(barrier, inc=1, device_id=device, device_id_type=MESH)
    pl.semaphore_wait(barrier, len(everyone))

    mine = pl.ds(pl.multiple_of(p * block, block), block)

    def input_copies(j):
        peer = (p + j) % size
        slot = jnp.maximum(peer - 1, 0)
        return [
            pltpu.make_async_remote_copy(
                src.at[slot], dst.at[mine], i_ss.at[n, j - 1], i_rs.at[n, j - 1],
                device_id=(g, peer), device_id_type=MESH,
            )
            for n, (src, dst) in enumerate(((in_hbm, x_ref), (cot_hbm, cot_ref)))
        ]

    def own_inputs():
        slot = jnp.maximum(p - 1, 0)
        return [
            pltpu.make_async_copy(src.at[slot], dst.at[mine], local.at[n])
            for n, (src, dst) in enumerate(((in_hbm, x_ref), (cot_hbm, cot_ref)))
        ]

    def wait_inputs(n):
        @pl.when(p > 0)
        def _():
            own_inputs()[n].wait()
            for j in range(1, size):
                input_copies(j)[n].wait_recv()

        for j in range(1, size):
            @pl.when((p + j) % size > 0)
            def _(j=j):
                input_copies(j)[n].wait_send()

    for n in range(2):
        for j in range(1, size):
            @pl.when((p + j) % size > 0)
            def _(j=j, n=n):
                input_copies(j)[n].start()

    @pl.when(p > 0)
    def _():
        for copy in own_inputs():
            copy.start()

    @pl.when(p == 0)
    def _():
        x_ref[...] = jnp.zeros(x_ref.shape, x_ref.dtype)
        cot_ref[...] = jnp.zeros(cot_ref.shape, cot_ref.dtype)

    slots, block, _ = out_ref.shape
    size = slots + 1

    def result_copies(j):
        peer = (p + j) % size
        slot = jnp.maximum(p - 1, 0)
        part = pl.ds(pl.multiple_of(peer * block, block), block)
        return [
            pltpu.make_async_remote_copy(
                src.at[part], dst.at[slot], o_ss.at[n, j - 1], o_rs.at[n, j - 1],
                device_id=(g, peer), device_id_type=MESH,
            )
            for n, (src, dst) in enumerate(((out_seq, out_ref), (grad_seq, gin_ref)))
        ]

    def own_results():
        part = pl.ds(pl.multiple_of(p * block, block), block)
        slot = jnp.maximum(p - 1, 0)
        return [
            pltpu.make_async_copy(out_seq.at[part], out_ref.at[slot], local.at[0]),
            pltpu.make_async_copy(grad_seq.at[part], gin_ref.at[slot], local.at[1]),
        ]

    def copy_d(c):
        return pltpu.make_async_remote_copy(
            give.at[c % 2], d_recv.at[c % SLOTS], d_ss.at[c % SLOTS], d_rs.at[c % SLOTS], device_id=sib, device_id_type=MESH
        )

    def copy_y(c):
        return pltpu.make_async_remote_copy(
            y_send.at[c % SLOTS], y_recv.at[c % SLOTS], y_ss.at[c % SLOTS], y_rs.at[c % SLOTS], device_id=ypeer, device_id_type=MESH
        )

    def copy_x(c):
        return pltpu.make_async_remote_copy(
            x_send.at[c % SLOTS], x_recv.at[c % SLOTS], x_ss.at[c % SLOTS], x_rs.at[c % SLOTS], device_id=xpeer, device_id_type=MESH
        )

    def part_of(k):
        return pl.ds(pl.multiple_of(k * piece, piece), piece)

    def copy_z(c, j):
        return pltpu.make_async_remote_copy(
            z_send.at[c % SLOTS, part_of((z + j) % ZED)], z_recv.at[c % SLOTS, j - 1], z_ss.at[c % SLOTS, j - 1], z_rs.at[c % SLOTS, j - 1],
            device_id=zpeer(j), device_id_type=MESH,
        )

    def copy_w(c, j):
        return pltpu.make_async_remote_copy(
            w_send.at[c % SLOTS], w_recv.at[c % SLOTS, j - 1], w_ss.at[c % SLOTS, j - 1], w_rs.at[c % SLOTS, j - 1],
            device_id=wpeer(j), device_id_type=MESH,
        )

    def copy_g(c, j):
        place = full.at[c, x, part_of(z)]
        return pltpu.make_async_remote_copy(
            place, place, g_ss.at[c, j - 1], g_rs.at[c, j - 1], device_id=zpeer(j), device_id_type=MESH
        )

    def copy_h(c):
        place = full.at[c, x]
        return pltpu.make_async_remote_copy(
            place, place, h_ss.at[c], h_rs.at[c], device_id=xpeer, device_id_type=MESH
        )

    def copy_s(c):
        u, s = c // subs, c % subs
        half = feat // 2
        return [
            pltpu.make_async_copy(
                full.at[c, h],
                sums_hbm.at[
                    pl.ds(pl.multiple_of(s * rows, rows), rows),
                    pl.ds(pl.multiple_of(u * feat + h * half, half), half),
                ],
                s_sem.at[c, h],
            )
            for h in range(2)
        ]

    def make(c):
        u, s = c // subs, c % subs

        def left_rows(q):
            down = feat * q + quarter * u
            rest = ff + feat * ((u >= 2 * tiles).astype(jnp.int32) + (u > 2 * tiles).astype(jnp.int32)) + quarter * q
            start = jnp.where(u < tiles, down, rest) + s * rows
            return left[pl.ds(pl.multiple_of(start, rows), rows), :]

        order = (2 * (1 - y) + core, 2 * y + core, 2 * (1 - y) + 1 - core, 2 * y + 1 - core)
        lhs = jnp.concatenate([left_rows(q) for q in order], axis=0)
        cols = pl.ds(pl.multiple_of(feat * jnp.maximum(u - tiles + 1, 0), feat), feat)
        total = jnp.dot(lhs, right[:, cols], preferred_element_type=F32)
        slot = c % 2
        own[slot, 0] = total[:rows]
        own[slot, 1] = total[rows : 2 * rows]
        give[slot, 0] = total[2 * rows : 3 * rows].astype(BF16)
        give[slot, 1] = total[3 * rows :].astype(BF16)
        copy_d(c).start()

    def stage_y(c):
        copy_d(c).wait()
        slot = c % 2
        y_send[c % SLOTS] = (own[slot, 0] + d_recv[c % SLOTS, 0].astype(F32)).astype(BF16)
        copy_y(c).start()
        y_keep[c % SLOTS] = own[slot, 1] + d_recv[c % SLOTS, 1].astype(F32)

    def stage_x(c):
        copy_y(c).wait()
        half = feat // 2
        total = y_keep[c % SLOTS] + y_recv[c % SLOTS].astype(F32)

        @pl.when(x == 0)
        def _():
            x_send[c % SLOTS] = total[:, half:].astype(BF16)
            x_keep[c % SLOTS] = total[:, :half]

        @pl.when(x == 1)
        def _():
            x_send[c % SLOTS] = total[:, :half].astype(BF16)
            x_keep[c % SLOTS] = total[:, half:]

        copy_x(c).start()

    def stage_z(c):
        copy_x(c).wait()
        total = x_keep[c % SLOTS] + x_recv[c % SLOTS].astype(F32)
        z_send[c % SLOTS] = total.astype(BF16)
        for j in range(1, ZED):
            copy_z(c, j).start()

    def add_z(c):
        for j in range(1, ZED):
            copy_z(c, j).wait()
        total = z_send[c % SLOTS, part_of(z)].astype(F32)
        for j in range(1, ZED):
            total = total + z_recv[c % SLOTS, j - 1].astype(F32)
        return total

    def stage_w(c):
        w_send[c % SLOTS] = add_z(c).astype(BF16)
        for j in range(1, groups):
            copy_w(c, j).start()

    def add_w(c):
        for j in range(1, groups):
            copy_w(c, j).wait()
        total = w_send[c % SLOTS].astype(F32)
        for j in range(1, groups):
            total = total + w_recv[c % SLOTS, j - 1].astype(F32)
        return total

    def stage_g(c):
        full[c, x, part_of(z)] = (add_z(c) if groups == 1 else add_w(c)).astype(BF16)
        for j in range(1, ZED):
            copy_g(c, j).start()

    def stage_h(c):
        for j in range(1, ZED):
            copy_g(c, j).wait()
        copy_h(c).start()

    def stage_s(c):
        copy_h(c).wait()
        for copy in copy_s(c):
            copy.start()

    ways = [[sib], [ypeer], [xpeer], [zpeer(j) for j in range(1, ZED)]]
    if groups > 1:
        ways.append([wpeer(j) for j in range(1, groups)])
    firsts = [sum(len(way) for way in ways[:i]) for i in range(len(ways))]

    def vector_copies(i):
        return [
            pltpu.make_async_remote_copy(
                vec_sum.at[i], vec_recv.at[firsts[i] + n], v_ss.at[firsts[i] + n], v_rs.at[firsts[i] + n],
                device_id=device, device_id_type=MESH,
            )
            for n, device in enumerate(ways[i])
        ]

    def vector_step(i):
        if i == 0:
            vec_sum[0] = vec_part[...]
        else:
            for copy in vector_copies(i - 1):
                copy.wait()
            total = vec_sum[i - 1]
            for n in range(len(ways[i - 1])):
                total = total + vec_recv[firsts[i - 1] + n]
            vec_sum[i] = total
        if i < len(ways):
            for copy in vector_copies(i):
                copy.start()

    stages = [make, stage_y, stage_x, stage_z] + ([stage_w] if groups > 1 else []) + [stage_g, stage_h, stage_s]
    offsets = [sum(lags[: i + 1]) for i in range(len(stages))]

    def step(t, carry):
        for stage, offset in zip(stages, offsets):
            c = t - offset

            @pl.when((c >= 0) & (c < chunks))
            def _(stage=stage, c=c):
                stage(c)

        return carry

    def run_steps(first, end):
        lax.fori_loop(first, end, step, 0)

    length = len_ref[jnp.maximum(p - 1, 0)]
    keys = lax.broadcasted_iota(jnp.int32, (seq, seq), 0)
    queries = lax.broadcasted_iota(jnp.int32, (seq, seq), 1)
    bias[...] = jnp.where((keys <= queries) & (keys < length), 0.0, -1e30).astype(F32)
    inside = (lax.broadcasted_iota(jnp.int32, (seq, 1), 0) < length).astype(F32)
    low_lanes = lax.broadcasted_iota(jnp.int32, (seq, half), 1) < HEAD

    def pick(values, head):
        zero = jnp.zeros_like(values)
        return jnp.where(low_lanes, values, zero) if head == 0 else jnp.where(low_lanes, zero, values)

    def rows_of(i):
        return pl.ds(i * seq, seq)

    def put_left(offset, i, values):
        left[pl.ds(offset, values.shape[1]), rows_of(i)] = values.T

    N2, CTX, N1 = ff, ff + feat, ff + 2 * feat
    HID, ATT, QKV = feat, feat + ff, 2 * feat + ff

    def forward(i):
        value = state[i]
        n1 = (normalize(value)[0] * gain1_ref[...] + shift1_ref[...]).astype(BF16)
        put_left(N1, i, n1)
        if i == 0:
            weight_copies[0].wait()
        for j in range(3):
            part = dot(n1, wqkv[:, j * feat : (j + 1) * feat])
            if j == 0:
                part = part * HEAD ** (-0.5)
            part = part.astype(BF16)
            qkv[i, :, j * feat : (j + 1) * feat] = part
            if j == 1:
                kt[i] = part.T
            if j == 2:
                vt[i] = part.T

        def pair(hp, carry):
            lanes = pl.ds(pl.multiple_of(hp * half, half), half)
            q2 = qkv[i, :, lanes]
            for head in range(2):
                qm = pick(q2, head)
                scores = []
                for b in range(i + 1):
                    k2 = qkv[b, :, pl.ds(pl.multiple_of(feat + hp * half, half), half)]
                    scores.append(dot_nt(k2, qm) + bias[...])
                top = jnp.max(scores[0], axis=0, keepdims=True)
                for s in scores[1:]:
                    top = jnp.maximum(top, jnp.max(s, axis=0, keepdims=True))
                weights = [jnp.exp(s - top) for s in scores]
                total = jnp.sum(weights[0], axis=0, keepdims=True)
                for w in weights[1:]:
                    total = total + jnp.sum(w, axis=0, keepdims=True)
                inv = 1.0 / total
                lse[i, pl.ds(2 * hp + head, 1), :] = top + jnp.log(total)
                rows = pl.ds(pl.multiple_of(hp * half + head * HEAD, HEAD), HEAD)
                acc = None
                for b in range(i + 1):
                    term = dot(vt[b, rows, :], (weights[b] * inv).astype(BF16))
                    acc = term if acc is None else acc + term
                left[pl.ds(pl.multiple_of(CTX + hp * half + head * HEAD, HEAD), HEAD), rows_of(i)] = acc.astype(BF16)
            return carry

        lax.fori_loop(0, feat // half, pair, 0)
        ctx[...] = left[pl.ds(CTX, feat), rows_of(i)].T
        if i == 0:
            weight_copies[1].wait()
        mix = state[i] + dot(ctx[...], wout[...])
        mixed[i] = mix
        n2 = (normalize(mix)[0] * gain2_ref[...] + shift2_ref[...]).astype(BF16)
        put_left(N2, i, n2)
        if i == 0:
            weight_copies[2].wait()
            weight_copies[3].wait()
        acc = mix
        for j in range(tiles):
            u = dot(n2, wup[:, j * feat : (j + 1) * feat])
            c = 0.7978845608028654
            square = u * u
            th = jnp.tanh(c * u * (1.0 + 0.044715 * square))
            halfp = 0.5 + 0.5 * th
            active = (u * halfp).astype(BF16)
            slope = halfp + 0.5 * u * (1.0 - th * th) * (c * (1.0 + 3 * 0.044715 * square))
            gp[i, :, j * feat : (j + 1) * feat] = slope.astype(BF16)
            put_left(j * feat, i, active)
            acc = acc + dot(active, wdown[j * feat : (j + 1) * feat, :])
        return acc

    def norm_back(values, d_out, gain, slot, first):
        norm, scale = normalize(values)
        g_gain = jnp.sum(d_out * norm, axis=0, keepdims=True)
        g_shift = jnp.sum(d_out, axis=0, keepdims=True)
        if first:
            vec_part[slot : slot + 1, :] = g_gain
            vec_part[slot + 1 : slot + 2, :] = g_shift
        else:
            vec_part[slot : slot + 1, :] += g_gain
            vec_part[slot + 1 : slot + 2, :] += g_shift
        t = d_out * gain
        return scale * (t - jnp.mean(t, axis=-1, keepdims=True) - norm * jnp.mean(t * norm, axis=-1, keepdims=True))

    def backward(i, grad):
        branch = grad.astype(BF16)
        right[rows_of(i), 0:feat] = branch
        if i == 0:
            run_steps(0, EARLY[0])
        acc = None
        for j in range(tiles):
            d_active = dot_nt(branch, wdown[j * feat : (j + 1) * feat, :])
            d_hidden = (d_active * gp[i, :, j * feat : (j + 1) * feat].astype(F32)).astype(BF16)
            right[rows_of(i), HID + j * feat : HID + (j + 1) * feat] = d_hidden
            term = dot_nt(d_hidden, wup[:, j * feat : (j + 1) * feat])
            acc = term if acc is None else acc + term
        if i == 0:
            run_steps(EARLY[0], EARLY[1])
        d_mixed = grad + norm_back(mixed[i], acc, gain2_ref[...], 2, i == 1)
        d_attn = d_mixed.astype(BF16)
        right[rows_of(i), ATT : ATT + feat] = d_attn
        dctx[...] = dot_nt(d_attn, wout[...]).astype(BF16)

        def pair(hp, carry):
            lanes = pl.ds(pl.multiple_of(hp * half, half), half)
            q2 = qkv[i, :, lanes]
            do2 = dctx[:, lanes]
            dk = [None] * (i + 1)
            dv = [None] * (i + 1)
            for head in range(2):
                qm = pick(q2, head)
                dom = pick(do2, head)
                row = lse[i, pl.ds(2 * hp + head, 1), :]
                soft, d_soft = [], []
                inner = None
                for b in range(i + 1):
                    k2 = qkv[b, :, pl.ds(pl.multiple_of(feat + hp * half, half), half)]
                    v2 = qkv[b, :, pl.ds(pl.multiple_of(2 * feat + hp * half, half), half)]
                    soft.append(jnp.exp(dot_nt(k2, qm) + (bias[...] - row)))
                    d_soft.append(dot_nt(v2, dom))
                    term = jnp.sum(soft[b] * d_soft[b], axis=0, keepdims=True)
                    inner = term if inner is None else inner + term
                rows = pl.ds(pl.multiple_of(hp * half + head * HEAD, HEAD), HEAD)
                dq = None
                for b in range(i + 1):
                    d_score = (soft[b] * (d_soft[b] - inner)).astype(BF16)
                    term_v = dot(soft[b].astype(BF16), dom)
                    term_k = dot(d_score, qm)
                    term_q = dot(kt[b, rows, :], d_score)
                    dv[b] = term_v if dv[b] is None else dv[b] + term_v
                    dk[b] = term_k if dk[b] is None else dk[b] + term_k
                    dq = term_q if dq is None else dq + term_q
                dqt[rows, :] = (dq * HEAD ** (-0.5)).astype(BF16)
            dk_own, dv_own = dk[i], dv[i]
            if i == 1:
                dk_more[:, lanes] = dk[0]
                dv_more[:, lanes] = dv[0]
            else:
                dk_own = dk_own + dk_more[:, lanes]
                dv_own = dv_own + dv_more[:, lanes]
            right[rows_of(i), pl.ds(pl.multiple_of(QKV + feat + hp * half, half), half)] = dk_own.astype(BF16)
            right[rows_of(i), pl.ds(pl.multiple_of(QKV + 2 * feat + hp * half, half), half)] = dv_own.astype(BF16)
            if i == 0:
                @pl.when(hp % 2 == 1)
                def _():
                    step(EARLY[1] + hp // 2, 0)
            return carry

        lax.fori_loop(0, feat // half, pair, 0)
        right[rows_of(i), QKV : QKV + feat] = dqt[...].T
        d_normed = None
        for j in range(3):
            term = dot_nt(
                right[rows_of(i), QKV + j * feat : QKV + (j + 1) * feat], wqkv[:, j * feat : (j + 1) * feat]
            )
            d_normed = term if d_normed is None else d_normed + term
        return d_mixed + norm_back(state[i], d_normed, gain1_ref[...], 0, i == 1)

    wait_inputs(0)
    state[0] = x_ref[...].astype(F32)
    first = forward(0)
    state[1] = first.astype(BF16).astype(F32) + embed_ref[...]
    second = forward(1)
    out_seq[...] = (second * inside).astype(BF16)
    wait_inputs(1)

    def send_results(n):
        @pl.when(p > 0)
        def _():
            for j in range(1, size):
                result_copies(j)[n].start()
            own_results()[n].start()

    send_results(0)
    d_carry = backward(1, cot_ref[...].astype(F32) * inside)
    vec_part[4:5, :] = jnp.sum(d_carry, axis=0, keepdims=True)
    vec_part[5:8, :] = jnp.zeros((3, feat), F32)
    d_state = backward(0, d_carry.astype(BF16).astype(F32))
    grad_seq[...] = d_state.astype(BF16)
    send_results(1)

    begun = EARLY[1] + 3
    vector_step(0)

    def late_step(t, carry):
        step(t, 0)
        for i in range(1, len(ways) + 1):
            @pl.when(t == begun + 3 * i)
            def _(i=i):
                vector_step(i)

        return carry

    lax.fori_loop(begun, chunks + offsets[-1], late_step, 0)
    vec_ref[...] = vec_sum[len(ways)]

    @pl.when(p > 0)
    def _():
        for copy in own_results():
            copy.wait()
        for j in range(1, size):
            for copy in result_copies(j):
                copy.wait_send()

    for j in range(1, size):
        source = (p + size - j) % size

        @pl.when(source > 0)
        def _(j=j, source=source):
            for n, dst in enumerate((out_ref, gin_ref)):
                pltpu.make_async_copy(dst.at[source - 1], dst.at[source - 1], o_rs.at[n, j - 1]).wait()

    def finish(c, carry):
        for copy in copy_s(c):
            copy.wait()
        return carry

    lax.fori_loop(0, chunks, finish, 0)


def run_block(inputs, cotangent, lengths, vectors, w_qkv, w_out, w_up, w_down, rows, lags, groups):
    slots, block, feat = inputs.shape
    ff = w_up.shape[1]
    seq = (slots + 1) * block
    quarter = feat // 4
    units = (2 * ff + 4 * feat) // feat
    chunks = units * (quarter // rows)
    piece = rows // ZED
    half = feat // 2
    ways = 4 + (groups > 1)
    landings = 6 + (groups - 1)
    more = max(groups - 1, 1)
    dma = pltpu.SemaphoreType.DMA
    local_block = jax.ShapeDtypeStruct((slots, block, feat), BF16)
    left_rows = ff + 3 * feat
    right_cols = 5 * feat + ff
    return pl.pallas_call(
        functools.partial(block_kernel, (rows, lags, groups)),
        out_shape=(
            jax.ShapeDtypeStruct((quarter, units * feat), BF16),
            local_block,
            local_block,
            jax.ShapeDtypeStruct((8, feat), F32),
        ),
        in_specs=[ANY, ANY, SMEM] + [VMEM] * 5 + [ANY] * 4,
        out_specs=(ANY, VMEM, VMEM, VMEM),
        scratch_shapes=[
            pltpu.VMEM((seq, feat), BF16),
            pltpu.VMEM((seq, feat), BF16),
            pltpu.VMEM((seq, feat), BF16),
            pltpu.VMEM((seq, feat), BF16),
            pltpu.VMEM((8, feat), F32),
            pltpu.VMEM((ways + 1, 8, feat), F32),
            pltpu.VMEM(w_qkv.shape, BF16),
            pltpu.VMEM(w_out.shape, BF16),
            pltpu.VMEM(w_up.shape, BF16),
            pltpu.VMEM(w_down.shape, BF16),
            pltpu.VMEM((left_rows, 2 * seq), BF16),
            pltpu.VMEM((2 * seq, right_cols), BF16),
            pltpu.VMEM((2, seq, 3 * feat), BF16),
            pltpu.VMEM((2, feat, seq), BF16),
            pltpu.VMEM((2, feat, seq), BF16),
            pltpu.VMEM((2, 16, seq), F32),
            pltpu.VMEM((2, seq, ff), BF16),
            pltpu.VMEM((2, seq, feat), F32),
            pltpu.VMEM((2, seq, feat), F32),
            pltpu.VMEM((seq, feat), BF16),
            pltpu.VMEM((seq, feat), F32),
            pltpu.VMEM((seq, feat), F32),
            pltpu.VMEM((feat, seq), BF16),
            pltpu.VMEM((seq, feat), BF16),
            pltpu.VMEM((seq, seq), F32),
            pltpu.VMEM((2, 2, rows, feat), F32),
            pltpu.VMEM((2, 2, rows, feat), BF16),
            pltpu.VMEM((SLOTS, 2, rows, feat), BF16),
            pltpu.VMEM((SLOTS, rows, feat), BF16),
            pltpu.VMEM((SLOTS, rows, feat), F32),
            pltpu.VMEM((SLOTS, rows, feat), BF16),
            pltpu.VMEM((SLOTS, rows, half), BF16),
            pltpu.VMEM((SLOTS, rows, half), F32),
            pltpu.VMEM((SLOTS, rows, half), BF16),
            pltpu.VMEM((SLOTS, rows, half), BF16),
            pltpu.VMEM((SLOTS, ZED - 1, piece, half), BF16),
            pltpu.VMEM((SLOTS if groups > 1 else 1, piece, half), BF16),
            pltpu.VMEM((SLOTS if groups > 1 else 1, more, piece, half), BF16),
            pltpu.VMEM((chunks, 2, rows, half), BF16),
            pltpu.VMEM((landings, 8, feat), F32),
            dma((4,)), dma((2, slots)), dma((2, slots)),
            dma((SLOTS,)), dma((SLOTS,)), dma((SLOTS,)), dma((SLOTS,)), dma((SLOTS,)), dma((SLOTS,)),
            dma((SLOTS, ZED - 1)), dma((SLOTS, ZED - 1)),
            dma((SLOTS, more)), dma((SLOTS, more)),
            dma((chunks, ZED - 1)), dma((chunks, ZED - 1)),
            dma((chunks,)), dma((chunks,)), dma((chunks, 2)),
            dma((2, slots)), dma((2, slots)), dma((landings,)), dma((landings,)), dma((2,)),
        ],
        compiler_params=pltpu.CompilerParams(
            collective_id=0, has_side_effects=True, vmem_limit_bytes=60 * 2**20
        ),
    )(inputs, cotangent, lengths, *vectors, w_qkv, w_out, w_up, w_down)


def shards(
    inputs, lengths, w_qkv, w_out, w_up, w_down, norm1_gain, norm1_shift, norm2_gain, norm2_shift, pass_embed, cotangent
):
    p = lax.axis_index("pipe")
    slots, block, feat = inputs.shape
    ff = w_up.shape[1]
    groups = lax.axis_size("dp") // (2 * ZED)
    vectors = [v.reshape(1, feat) for v in (norm1_gain, norm1_shift, norm2_gain, norm2_shift, pass_embed)]
    sums, block_out, input_grads, vec = run_block(
        inputs, cotangent, lengths, vectors, w_qkv, w_out, w_up, w_down, ROWS, LAGS[: 7 + (groups > 1)], groups
    )
    quarter = feat // 4
    tiles = ff // feat
    down = jnp.concatenate([sums[:, j * feat : (j + 1) * feat] for j in range(tiles)], axis=0).astype(F32)
    up = sums[:, ff : 2 * ff].astype(F32)
    out = sums[:, 2 * ff : 2 * ff + feat].astype(F32)
    qkv = sums[:, 2 * ff + feat :].astype(F32)
    vector = lax.dynamic_slice_in_dim(vec, p * quarter, quarter, 1)
    return (block_out, input_grads, qkv, out, up, down) + tuple(vector[i] for i in range(5))


def solution(mesh):
    rep = P()
    seqs = P("dp", "pipe", None)
    return jax.shard_map(
        shards,
        mesh=mesh,
        in_specs=(seqs, P("dp")) + (rep,) * 9 + (seqs,),
        out_specs=(seqs, seqs) + (P("pipe", None),) * 4 + (P("pipe"),) * 5,
        check_vma=False,
    )
```

time: 209 us -> 178 us (0.85)
  Pallas kernels: 188 us -> 158 us
  local copies, waits for them, and re-layouts: 12.2 us -> 9.33 us
  other arithmetic: 6.82 us -> 9.25 us
    pallas_call x3 -> x1, Pallas kernels: 188 us -> 158 us  [run_block(): pl.pallas_call(functools.partial(block_kernel, (rows, lags, groups)), out...]
where the time goes in v2:
time: 178 us; the launch traced here: 177 us
  Pallas kernels  158 us (89%)
  local copies, waits for them, and re-layouts  9.33 us (5%)
  other arithmetic  9.25 us (5%)
    pallas_call x1, Pallas kernels, run_block(): pl.pallas_call(functools.partial(block_kernel, (rows, lags, groups)), out...  158 us
    reshape x5, local copies, waits for them, and re-layouts, shards(): v.reshape(1, feat)  6.33 us

profile of v2, /device:TPU:0, one launch (start us, length us, event | category | flops | bytes accessed | tf_op | source)
XLA Modules:
  0.0 177.1 jit_solution(428796815737481125)
XLA Ops:
  0.6 1.3 reshape.37.gain1_ref
  1.9 1.3 reshape.38.shift1_ref
  3.2 1.3 reshape.39.gain2_ref
  4.4 1.3 reshape.40.shift2_ref
  5.7 1.3 reshape.41.embed_ref
  7.0 157.9 %shard_map.203 = (bf16[192,9216]{1,0:T(8,128)(2,1)}, bf16[3,64,768]{2,1,0:T(8,128)(2,1)}, bf16[3,64,768]{2,1,0:T(8,128)(2,1)}, f32[8,768]{1,0:T(8,128)}) custom-call(bf16[3,64,768]{2,1,0:T(8,128)(2,1)} %in_hbm.1, bf16[3,64,768]{2,1,0:T(8,128)(2,1)} %cot_hbm.1, s32[3]{0:T(128)} %len_ref.1, f32[1,768]{1,0:T(1,128)} %reshape.37.gain1_ref, ...), custom_call_target="tpu_custom_call" | custom-call | tf_op jit(solution)/shard_map/pallas_call | solution.py:608
  164.9 1.6 fusion.1
  166.4 2.5 %slice_convert_fusion.1 = f32[192,2304]{1,0:T(8,128)} fusion(bf16[192,9216]{1,0:T(8,128)(2,1)} %get-tuple-element.17), kind=kLoop, calls=%fused_computation.2 | loop fusion | flops 442368 | bytes 2654208 | tf_op jit(solution)/shard_map/convert_element_type | solution.py:689
  168.9 2.3 %fusion = (bf16[192,768]{1,0:T(8,128)(2,1)S(1)}, bf16[192,768]{1,0:T(8,128)(2,1)S(1)}, bf16[192,768]{1,0:T(8,128)(2,1)S(1)}, bf16[192,768]{1,0:T(8,128)(2,1)S(1)}, f32[192,768]{1,0:T(8,128)}) fusion(bf16[192,9216]{1,0:T(8,128)(2,1)} %get-tuple-element.17), kind=kLoop, calls=%fused_computation.5 | loop fusion | flops 147456 | bytes 3244032 | tf_op jit(solution)/shard_map/slice | solution.py:686
  171.2 2.9 %slice_convert_fusion = f32[192,3072]{1,0:T(8,128)} fusion(bf16[192,9216]{1,0:T(8,128)(2,1)} %get-tuple-element.17), kind=kLoop, calls=%fused_computation.1 | loop fusion | flops 589824 | bytes 3538944 | tf_op jit(solution)/shard_map/convert_element_type | solution.py:687
  174.1 0.0 copy-start.1
  174.1 0.0 copy-start
  174.1 1.6 maximum_convert_fusion
  175.7 0.0 copy-done.1
  175.7 0.7 copy.25
  176.4 0.0 copy-done
  176.4 0.7 copy.26
Async XLA Ops:
  174.1 1.6 copy-start.1
  174.1 2.3 %copy-start = (bf16[3,64,768]{2,1,0:T(8,128)(2,1)S(1)}, bf16[3,64,768]{2,1,0:T(8,128)(2,1)}, u32[]{:S(2)}) copy-start(bf16[3,64,768]{2,1,0:T(8,128)(2,1)} %get-tuple-element.41) | copy-start | bytes 884740

commit v3 on v2

--- a/solution.py
+++ b/solution.py
@@ -25,6 +25,10 @@
     return lax.dot_general(left, right, (((1,), (1,)), ((), ())), preferred_element_type=F32)
 
 
+def row(ref):
+    return ref[...].reshape(1, ref.shape[0])
+
+
 def normalize(values):
     center = values - jnp.mean(values, axis=-1, keepdims=True)
     scale = lax.rsqrt(jnp.mean(center * center, axis=-1, keepdims=True) + 1e-05)
@@ -33,13 +37,16 @@
 
 ZED = 4
 SLOTS = 8
+STORES = 4
 ROWS = 64
 LAGS = (0, 1, 3, 2, 3, 3, 2, 2)
 EARLY = (2, 4)
+FORWARD_PAIRS = 3
+BACKWARD_PAIRS = 2
 
 
 def block_kernel(
-    dims, in_hbm, cot_hbm, len_ref, gain1_ref, shift1_ref, gain2_ref, shift2_ref, embed_ref,
+    dims, in_ref, given_ref, len_ref, gain1_ref, shift1_ref, gain2_ref, shift2_ref, embed_ref,
     wqkv_hbm, wout_hbm, wup_hbm, wdown_hbm,
     sums_hbm, out_ref, gin_ref, vec_ref,
     x_ref, cot_ref, out_seq, grad_seq, vec_part, vec_sum,
@@ -51,7 +58,7 @@
     o_ss, o_rs, v_ss, v_rs, local,
 ):
     rows, lags, groups = dims
-    slots, block, feat = in_hbm.shape
+    slots, block, feat = in_ref.shape
     size = slots + 1
     seq = size * block
     ff = wup.shape[1]
@@ -103,14 +110,14 @@
                 src.at[slot], dst.at[mine], i_ss.at[n, j - 1], i_rs.at[n, j - 1],
                 device_id=(g, peer), device_id_type=MESH,
             )
-            for n, (src, dst) in enumerate(((in_hbm, x_ref), (cot_hbm, cot_ref)))
+            for n, (src, dst) in enumerate(((in_ref, x_ref), (given_ref, cot_ref)))
         ]
 
     def own_inputs():
         slot = jnp.maximum(p - 1, 0)
         return [
             pltpu.make_async_copy(src.at[slot], dst.at[mine], local.at[n])
-            for n, (src, dst) in enumerate(((in_hbm, x_ref), (cot_hbm, cot_ref)))
+            for n, (src, dst) in enumerate(((in_ref, x_ref), (given_ref, cot_ref)))
         ]
 
     def wait_inputs(n):
@@ -197,13 +204,13 @@
     def copy_g(c, j):
         place = full.at[c, x, part_of(z)]
         return pltpu.make_async_remote_copy(
-            place, place, g_ss.at[c, j - 1], g_rs.at[c, j - 1], device_id=zpeer(j), device_id_type=MESH
+            place, place, g_ss.at[c % SLOTS, j - 1], g_rs.at[c % SLOTS, j - 1], device_id=zpeer(j), device_id_type=MESH
         )
 
     def copy_h(c):
         place = full.at[c, x]
         return pltpu.make_async_remote_copy(
-            place, place, h_ss.at[c], h_rs.at[c], device_id=xpeer, device_id_type=MESH
+            place, place, h_ss.at[c % SLOTS], h_rs.at[c % SLOTS], device_id=xpeer, device_id_type=MESH
         )
 
     def copy_s(c):
@@ -216,7 +223,7 @@
                     pl.ds(pl.multiple_of(s * rows, rows), rows),
                     pl.ds(pl.multiple_of(u * feat + h * half, half), half),
                 ],
-                s_sem.at[c, h],
+                s_sem.at[c % STORES, h],
             )
             for h in range(2)
         ]
@@ -305,6 +312,12 @@
 
     def stage_s(c):
         copy_h(c).wait()
+
+        @pl.when(c >= STORES)
+        def _():
+            for copy in copy_s(c - STORES):
+                copy.wait()
+
         for copy in copy_s(c):
             copy.start()
 
@@ -374,7 +387,7 @@
 
     def forward(i):
         value = state[i]
-        n1 = (normalize(value)[0] * gain1_ref[...] + shift1_ref[...]).astype(BF16)
+        n1 = (normalize(value)[0] * row(gain1_ref) + row(shift1_ref)).astype(BF16)
         put_left(N1, i, n1)
         if i == 0:
             weight_copies[0].wait()
@@ -389,39 +402,52 @@
             if j == 2:
                 vt[i] = part.T
 
-        def pair(hp, carry):
-            lanes = pl.ds(pl.multiple_of(hp * half, half), half)
-            q2 = qkv[i, :, lanes]
-            for head in range(2):
-                qm = pick(q2, head)
-                scores = []
-                for b in range(i + 1):
-                    k2 = qkv[b, :, pl.ds(pl.multiple_of(feat + hp * half, half), half)]
-                    scores.append(dot_nt(k2, qm) + bias[...])
-                top = jnp.max(scores[0], axis=0, keepdims=True)
-                for s in scores[1:]:
-                    top = jnp.maximum(top, jnp.max(s, axis=0, keepdims=True))
-                weights = [jnp.exp(s - top) for s in scores]
-                total = jnp.sum(weights[0], axis=0, keepdims=True)
-                for w in weights[1:]:
-                    total = total + jnp.sum(w, axis=0, keepdims=True)
-                inv = 1.0 / total
+        def group(first_pair, carry):
+            mid = seq // 2
+            heads = [(u, head) for u in range(FORWARD_PAIRS) for head in range(2)]
+            scores = []
+            for u, head in heads:
+                hp = first_pair * FORWARD_PAIRS + u
+                qm = pick(qkv[i, :, pl.ds(pl.multiple_of(hp * half, half), half)], head)
+                scores.append([
+                    dot_nt(qkv[b, :, pl.ds(pl.multiple_of(feat + hp * half, half), half)], qm)
+                    for b in range(i + 1)
+                ])
+            weights, invs = [], []
+            for n, (u, head) in enumerate(heads):
+                hp = first_pair * FORWARD_PAIRS + u
+                low = [s[:mid, :mid] + bias[:mid, :mid] for s in scores[n]]
+                high = [s[:, mid:] + bias[:, mid:] for s in scores[n]]
+                parts = []
+                stats = []
+                for blocks in (low, high):
+                    top = functools.reduce(jnp.maximum, [jnp.max(s, axis=0, keepdims=True) for s in blocks])
+                    w = [jnp.exp(s - top) for s in blocks]
+                    total = sum(jnp.sum(v, axis=0, keepdims=True) for v in w)
+                    parts.append([v.astype(BF16) for v in w])
+                    stats.append((top, total))
+                top = jnp.concatenate([stats[0][0], stats[1][0]], axis=1)
+                total = jnp.concatenate([stats[0][1], stats[1][1]], axis=1)
                 lse[i, pl.ds(2 * hp + head, 1), :] = top + jnp.log(total)
+                zero = jnp.zeros((mid, mid), BF16)
+                weights.append([
+                    jnp.concatenate([jnp.concatenate([lo, zero], axis=0), hi], axis=1) for lo, hi in zip(*parts)
+                ])
+                invs.append(1.0 / total)
+            for n, (u, head) in enumerate(heads):
+                hp = first_pair * FORWARD_PAIRS + u
                 rows = pl.ds(pl.multiple_of(hp * half + head * HEAD, HEAD), HEAD)
-                acc = None
-                for b in range(i + 1):
-                    term = dot(vt[b, rows, :], (weights[b] * inv).astype(BF16))
-                    acc = term if acc is None else acc + term
+                acc = sum(dot(vt[b, rows, :], weights[n][b]) for b in range(i + 1)) * invs[n]
                 left[pl.ds(pl.multiple_of(CTX + hp * half + head * HEAD, HEAD), HEAD), rows_of(i)] = acc.astype(BF16)
             return carry
 
-        lax.fori_loop(0, feat // half, pair, 0)
+        lax.fori_loop(0, feat // half // FORWARD_PAIRS, group, 0)
         ctx[...] = left[pl.ds(CTX, feat), rows_of(i)].T
         if i == 0:
             weight_copies[1].wait()
         mix = state[i] + dot(ctx[...], wout[...])
         mixed[i] = mix
-        n2 = (normalize(mix)[0] * gain2_ref[...] + shift2_ref[...]).astype(BF16)
+        n2 = (normalize(mix)[0] * row(gain2_ref) + row(shift2_ref)).astype(BF16)
         put_left(N2, i, n2)
         if i == 0:
             weight_copies[2].wait()
@@ -467,57 +493,69 @@
             acc = term if acc is None else acc + term
         if i == 0:
             run_steps(EARLY[0], EARLY[1])
-        d_mixed = grad + norm_back(mixed[i], acc, gain2_ref[...], 2, i == 1)
+        d_mixed = grad + norm_back(mixed[i], acc, row(gain2_ref), 2, i == 1)
         d_attn = d_mixed.astype(BF16)
         right[rows_of(i), ATT : ATT + feat] = d_attn
         dctx[...] = dot_nt(d_attn, wout[...]).astype(BF16)
 
-        def pair(hp, carry):
-            lanes = pl.ds(pl.multiple_of(hp * half, half), half)
-            q2 = qkv[i, :, lanes]
-            do2 = dctx[:, lanes]
-            dk = [None] * (i + 1)
-            dv = [None] * (i + 1)
-            for head in range(2):
-                qm = pick(q2, head)
-                dom = pick(do2, head)
-                row = lse[i, pl.ds(2 * hp + head, 1), :]
-                soft, d_soft = [], []
-                inner = None
-                for b in range(i + 1):
-                    k2 = qkv[b, :, pl.ds(pl.multiple_of(feat + hp * half, half), half)]
-                    v2 = qkv[b, :, pl.ds(pl.multiple_of(2 * feat + hp * half, half), half)]
-                    soft.append(jnp.exp(dot_nt(k2, qm) + (bias[...] - row)))
-                    d_soft.append(dot_nt(v2, dom))
-                    term = jnp.sum(soft[b] * d_soft[b], axis=0, keepdims=True)
-                    inner = term if inner is None else inner + term
-                rows = pl.ds(pl.multiple_of(hp * half + head * HEAD, HEAD), HEAD)
-                dq = None
-                for b in range(i + 1):
-                    d_score = (soft[b] * (d_soft[b] - inner)).astype(BF16)
-                    term_v = dot(soft[b].astype(BF16), dom)
-                    term_k = dot(d_score, qm)
-                    term_q = dot(kt[b, rows, :], d_score)
-                    dv[b] = term_v if dv[b] is None else dv[b] + term_v
-                    dk[b] = term_k if dk[b] is None else dk[b] + term_k
-                    dq = term_q if dq is None else dq + term_q
-                dqt[rows, :] = (dq * HEAD ** (-0.5)).astype(BF16)
-            dk_own, dv_own = dk[i], dv[i]
-            if i == 1:
-                dk_more[:, lanes] = dk[0]
-                dv_more[:, lanes] = dv[0]
-            else:
-                dk_own = dk_own + dk_more[:, lanes]
-                dv_own = dv_own + dv_more[:, lanes]
-            right[rows_of(i), pl.ds(pl.multiple_of(QKV + feat + hp * half, half), half)] = dk_own.astype(BF16)
-            right[rows_of(i), pl.ds(pl.multiple_of(QKV + 2 * feat + hp * half, half), half)] = dv_own.astype(BF16)
+        def group(first_pair, carry):
+            mid = seq // 2
+            for u in range(BACKWARD_PAIRS):
+                hp = first_pair * BACKWARD_PAIRS + u
+                lanes = pl.ds(pl.multiple_of(hp * half, half), half)
+                q2 = qkv[i, :, lanes]
+                do2 = dctx[:, lanes]
+                dk = [None] * (i + 1)
+                dv = [None] * (i + 1)
+                zero = jnp.zeros((mid, mid), BF16)
+                for head in range(2):
+                    qm = pick(q2, head)
+                    dom = pick(do2, head)
+                    lrow = lse[i, pl.ds(2 * hp + head, 1), :]
+                    soft = [[], []]
+                    d_soft = [[], []]
+                    for b in range(i + 1):
+                        k2 = qkv[b, :, pl.ds(pl.multiple_of(feat + hp * half, half), half)]
+                        v2 = qkv[b, :, pl.ds(pl.multiple_of(2 * feat + hp * half, half), half)]
+                        s = dot_nt(k2, qm)
+                        d = dot_nt(v2, dom)
+                        soft[0].append(jnp.exp(s[:mid, :mid] + (bias[:mid, :mid] - lrow[:, :mid])))
+                        soft[1].append(jnp.exp(s[:, mid:] + (bias[:, mid:] - lrow[:, mid:])))
+                        d_soft[0].append(d[:mid, :mid])
+                        d_soft[1].append(d[:, mid:])
+                    inner = [
+                        sum(jnp.sum(a * c, axis=0, keepdims=True) for a, c in zip(soft[h], d_soft[h])) for h in range(2)
+                    ]
+                    rows = pl.ds(pl.multiple_of(hp * half + head * HEAD, HEAD), HEAD)
+                    dq = None
+
+                    def whole(lo, hi):
+                        return jnp.concatenate([jnp.concatenate([lo, zero], axis=0), hi], axis=1)
+
+                    for b in range(i + 1):
+                        d_score = whole(*[(soft[h][b] * (d_soft[h][b] - inner[h])).astype(BF16) for h in range(2)])
+                        prob = whole(*[soft[h][b].astype(BF16) for h in range(2)])
+                        term_v = dot(prob, dom)
+                        term_k = dot(d_score, qm)
+                        term_q = dot(kt[b, rows, :], d_score)
+                        dv[b] = term_v if dv[b] is None else dv[b] + term_v
+                        dk[b] = term_k if dk[b] is None else dk[b] + term_k
+                        dq = term_q if dq is None else dq + term_q
+                    dqt[rows, :] = (dq * HEAD ** (-0.5)).astype(BF16)
+                dk_own, dv_own = dk[i], dv[i]
+                if i == 1:
+                    dk_more[:, lanes] = dk[0]
+                    dv_more[:, lanes] = dv[0]
+                else:
+                    dk_own = dk_own + dk_more[:, lanes]
+                    dv_own = dv_own + dv_more[:, lanes]
+                right[rows_of(i), pl.ds(pl.multiple_of(QKV + feat + hp * half, half), half)] = dk_own.astype(BF16)
+                right[rows_of(i), pl.ds(pl.multiple_of(QKV + 2 * feat + hp * half, half), half)] = dv_own.astype(BF16)
             if i == 0:
-                @pl.when(hp % 2 == 1)
-                def _():
-                    step(EARLY[1] + hp // 2, 0)
+                step(EARLY[1] + first_pair, 0)
             return carry
 
-        lax.fori_loop(0, feat // half, pair, 0)
+        lax.fori_loop(0, feat // half // BACKWARD_PAIRS, group, 0)
         right[rows_of(i), QKV : QKV + feat] = dqt[...].T
         d_normed = None
         for j in range(3):
@@ -525,12 +563,12 @@
                 right[rows_of(i), QKV + j * feat : QKV + (j + 1) * feat], wqkv[:, j * feat : (j + 1) * feat]
             )
             d_normed = term if d_normed is None else d_normed + term
-        return d_mixed + norm_back(state[i], d_normed, gain1_ref[...], 0, i == 1)
+        return d_mixed + norm_back(state[i], d_normed, row(gain1_ref), 0, i == 1)
 
     wait_inputs(0)
     state[0] = x_ref[...].astype(F32)
     first = forward(0)
-    state[1] = first.astype(BF16).astype(F32) + embed_ref[...]
+    state[1] = first.astype(BF16).astype(F32) + row(embed_ref)
     second = forward(1)
     out_seq[...] = (second * inside).astype(BF16)
     wait_inputs(1)
@@ -550,7 +588,7 @@
     grad_seq[...] = d_state.astype(BF16)
     send_results(1)
 
-    begun = EARLY[1] + 3
+    begun = EARLY[1] + feat // half // BACKWARD_PAIRS
     vector_step(0)
 
     def late_step(t, carry):
@@ -586,7 +624,7 @@
             copy.wait()
         return carry
 
-    lax.fori_loop(0, chunks, finish, 0)
+    lax.fori_loop(chunks - STORES, chunks, finish, 0)
 
 
 def run_block(inputs, cotangent, lengths, vectors, w_qkv, w_out, w_up, w_down, rows, lags, groups):
@@ -613,7 +651,7 @@
             local_block,
             jax.ShapeDtypeStruct((8, feat), F32),
         ),
-        in_specs=[ANY, ANY, SMEM] + [VMEM] * 5 + [ANY] * 4,
+        in_specs=[VMEM, VMEM, SMEM] + [VMEM] * 5 + [ANY] * 4,
         out_specs=(ANY, VMEM, VMEM, VMEM),
         scratch_shapes=[
             pltpu.VMEM((seq, feat), BF16),
@@ -659,9 +697,9 @@
             dma((4,)), dma((2, slots)), dma((2, slots)),
             dma((SLOTS,)), dma((SLOTS,)), dma((SLOTS,)), dma((SLOTS,)), dma((SLOTS,)), dma((SLOTS,)),
             dma((SLOTS, ZED - 1)), dma((SLOTS, ZED - 1)),
-            dma((SLOTS, more)), dma((SLOTS, more)),
-            dma((chunks, ZED - 1)), dma((chunks, ZED - 1)),
-            dma((chunks,)), dma((chunks,)), dma((chunks, 2)),
+            dma((SLOTS if groups > 1 else 1, more)), dma((SLOTS if groups > 1 else 1, more)),
+            dma((SLOTS, ZED - 1)), dma((SLOTS, ZED - 1)),
+            dma((SLOTS,)), dma((SLOTS,)), dma((STORES, 2)),
             dma((2, slots)), dma((2, slots)), dma((landings,)), dma((landings,)), dma((2,)),
         ],
         compiler_params=pltpu.CompilerParams(
@@ -670,25 +708,82 @@
     )(inputs, cotangent, lengths, *vectors, w_qkv, w_out, w_up, w_down)
 
 
+def finish_kernel(
+    sums_hbm, block_ref, grads_ref, vec_ref,
+    block_out, grads_out, qkv_out, out_out, up_out, down_out, gain1_out, shift1_out, gain2_out, shift2_out, embed_out,
+    low, high, l_sem, s_sem, c_sem,
+):
+    feat = vec_ref.shape[1]
+    quarter = feat // 4
+    units, tiles = low.shape[0], up_out.shape[1] // feat
+    passed = [
+        pltpu.make_async_copy(block_ref, block_out, c_sem.at[0]),
+        pltpu.make_async_copy(grads_ref, grads_out, c_sem.at[1]),
+    ]
+    loads = [
+        pltpu.make_async_copy(sums_hbm.at[:, pl.ds(u * feat, feat)], low.at[u], l_sem.at[u]) for u in range(units)
+    ]
+    for copy in loads + passed:
+        copy.start()
+    vec = pltpu.roll(vec_ref[...], feat - quarter * lax.axis_index("pipe"), 1)
+    for n, ref in enumerate((gain1_out, shift1_out, gain2_out, shift2_out, embed_out)):
+        ref[...] = vec[n, :quarter]
+    stores = []
+    for u in range(units):
+        loads[u].wait()
+        high[u] = low[u].astype(F32)
+        if u < tiles:
+            place = down_out.at[pl.ds(u * quarter, quarter)]
+        elif u < 2 * tiles:
+            place = up_out.at[:, pl.ds((u - tiles) * feat, feat)]
+        elif u == 2 * tiles:
+            place = out_out
+        else:
+            place = qkv_out.at[:, pl.ds((u - 2 * tiles - 1) * feat, feat)]
+        copy = pltpu.make_async_copy(high.at[u], place, s_sem.at[u])
+        copy.start()
+        stores.append(copy)
+    for copy in stores + passed:
+        copy.wait()
+
+
+def run_finish(sums, block_out, input_grads, vec, ff):
+    feat = vec.shape[1]
+    quarter = feat // 4
+    units = sums.shape[1] // feat
+    dma = pltpu.SemaphoreType.DMA
+
+    def result(*shape):
+        return jax.ShapeDtypeStruct(shape, F32)
+
+    return pl.pallas_call(
+        finish_kernel,
+        out_shape=(
+            jax.ShapeDtypeStruct(block_out.shape, BF16),
+            jax.ShapeDtypeStruct(input_grads.shape, BF16),
+            result(quarter, 3 * feat), result(quarter, feat), result(quarter, ff), result(ff // 4, feat),
+        ) + (result(quarter),) * 5,
+        in_specs=[ANY, VMEM, VMEM, VMEM],
+        out_specs=(ANY,) * 6 + (VMEM,) * 5,
+        scratch_shapes=[
+            pltpu.VMEM((units, quarter, feat), BF16),
+            pltpu.VMEM((units, quarter, feat), F32),
+            dma((units,)), dma((units,)), dma((2,)),
+        ],
+        compiler_params=pltpu.CompilerParams(vmem_limit_bytes=60 * 2**20),
+    )(sums, block_out, input_grads, vec)
+
+
 def shards(
     inputs, lengths, w_qkv, w_out, w_up, w_down, norm1_gain, norm1_shift, norm2_gain, norm2_shift, pass_embed, cotangent
 ):
-    p = lax.axis_index("pipe")
-    slots, block, feat = inputs.shape
     ff = w_up.shape[1]
     groups = lax.axis_size("dp") // (2 * ZED)
-    vectors = [v.reshape(1, feat) for v in (norm1_gain, norm1_shift, norm2_gain, norm2_shift, pass_embed)]
+    vectors = (norm1_gain, norm1_shift, norm2_gain, norm2_shift, pass_embed)
     sums, block_out, input_grads, vec = run_block(
         inputs, cotangent, lengths, vectors, w_qkv, w_out, w_up, w_down, ROWS, LAGS[: 7 + (groups > 1)], groups
     )
-    quarter = feat // 4
-    tiles = ff // feat
-    down = jnp.concatenate([sums[:, j * feat : (j + 1) * feat] for j in range(tiles)], axis=0).astype(F32)
-    up = sums[:, ff : 2 * ff].astype(F32)
-    out = sums[:, 2 * ff : 2 * ff + feat].astype(F32)
-    qkv = sums[:, 2 * ff + feat :].astype(F32)
-    vector = lax.dynamic_slice_in_dim(vec, p * quarter, quarter, 1)
-    return (block_out, input_grads, qkv, out, up, down) + tuple(vector[i] for i in range(5))
+    return run_finish(sums, block_out, input_grads, vec, ff)
 
 
 def solution(mesh):

time: 178 us -> 154 us (0.87)
  local copies, waits for them, and re-layouts: 9.33 us -> 0 us
  other arithmetic: 9.25 us -> 0 us
  Pallas kernels: 158 us -> 153 us
    pallas_call x1, Pallas kernels: 158 us -> 147 us  [run_block(): pl.pallas_call(functools.partial(block_kernel, (rows, lags, groups)), out...]
    convert_element_type x3 -> x0, other arithmetic: 7 us -> none  [the longest x1 2.93 us: shards(): up = sums[:, ff:2 * ff].astype(F32)]
    reshape x5 -> x0, local copies, waits for them, and re-layouts: 6.33 us -> none  [shards(): v.reshape(1, feat)]
    pallas_call x0 -> x1, Pallas kernels: none -> 5.96 us  [run_finish(): pl.pallas_call(finish_kernel, out_shape=(jax.ShapeDtypeStruct(block_out.s...]
    slice x1 -> x0, other arithmetic: 2.26 us -> none  [shards(): sums[:, j * feat:(j + 1) * feat]]
where the time goes in v3:
time: 154 us
  Pallas kernels  153 us (99%)
    pallas_call x1, Pallas kernels, run_block(): pl.pallas_call(functools.partial(block_kernel, (rows, lags, groups)), out...  147 us
    pallas_call x1, Pallas kernels, run_finish(): pl.pallas_call(finish_kernel, out_shape=(jax.ShapeDtypeStruct(block_out.s...  5.96 us

profile of v3, /device:TPU:0, one launch (start us, length us, event | category | flops | bytes accessed | tf_op | source)
XLA Modules:
  0.0 154.1 jit_solution(16393829600524276306)
XLA Ops:
  0.6 147.3 %shard_map.203 = (bf16[192,9216]{1,0:T(8,128)(2,1)}, bf16[3,64,768]{2,1,0:T(8,128)(2,1)}, bf16[3,64,768]{2,1,0:T(8,128)(2,1)}, f32[8,768]{1,0:T(8,128)}) custom-call(bf16[3,64,768]{2,1,0:T(8,128)(2,1)} %in_ref.1, bf16[3,64,768]{2,1,0:T(8,128)(2,1)} %given_ref.1, s32[3]{0:T(128)} %len_ref.1, f32[768]{0:T(1024)} %gain1_ref.1, f32[768]{0:T(1024)} %shift1_ref.1, ...), custom_call_target="tpu_custom_call" | custom-call | tf_op jit(solution)/shard_map/pallas_call | solution.py:646
  148.0 6.0 %shard_map.204 = (bf16[3,64,768]{2,1,0:T(8,128)(2,1)}, bf16[3,64,768]{2,1,0:T(8,128)(2,1)}, f32[192,2304]{1,0:T(8,128)}, f32[192,768]{1,0:T(8,128)}, f32[192,307...) custom-call(bf16[192,9216]{1,0:T(8,128)(2,1)} %get-tuple-element.15., ...), custom_call_target="tpu_custom_call" | custom-call | tf_op jit(solution)/shard_map/pallas_call | solution.py:759

commit v4 on v3

--- a/solution.py
+++ b/solution.py
@@ -37,28 +37,27 @@
 
 ZED = 4
 SLOTS = 8
-STORES = 4
 ROWS = 64
-LAGS = (0, 1, 3, 2, 3, 3, 2, 2)
-EARLY = (2, 4)
-FORWARD_PAIRS = 3
-BACKWARD_PAIRS = 2
+LAGS = (0, 1, 2, 2, 2, 2, 2, 2)
+EARLY = (3, 6)
+FORWARD_PAIRS = 6
+BACKWARD_PAIRS = (1, 6)
 
 
 def block_kernel(
-    dims, in_ref, given_ref, len_ref, gain1_ref, shift1_ref, gain2_ref, shift2_ref, embed_ref,
+    dims, in_hbm, given_hbm, len_ref, gain1_ref, shift1_ref, gain2_ref, shift2_ref, embed_ref,
     wqkv_hbm, wout_hbm, wup_hbm, wdown_hbm,
     sums_hbm, out_ref, gin_ref, vec_ref,
-    x_ref, cot_ref, out_seq, grad_seq, vec_part, vec_sum,
+    in_ref, given_ref, x_ref, cot_ref, out_seq, grad_seq, vec_part, vec_sum,
     wqkv, wout, wup, wdown, left, right, qkv, vt, kt, lse, gp, mixed, state, ctx,
     dk_more, dv_more, dqt, dctx, bias,
     own, give, d_recv, y_send, y_keep, y_recv, x_send, x_keep, x_recv,
     z_send, z_recv, w_send, w_recv, full, vec_recv,
-    w_sem, i_ss, i_rs, d_ss, d_rs, y_ss, y_rs, x_ss, x_rs, z_ss, z_rs, w_ss, w_rs, g_ss, g_rs, h_ss, h_rs, s_sem,
+    a_sem, w_sem, i_ss, i_rs, d_ss, d_rs, y_ss, y_rs, x_ss, x_rs, z_ss, z_rs, w_ss, w_rs, g_ss, g_rs, h_ss, h_rs, s_sem,
     o_ss, o_rs, v_ss, v_rs, local,
 ):
     rows, lags, groups = dims
-    slots, block, feat = in_ref.shape
+    slots, block, feat = in_hbm.shape
     size = slots + 1
     seq = size * block
     ff = wup.shape[1]
@@ -84,8 +83,17 @@
     def wpeer(j):
         return (g + 2 * ZED * ((w + j) % groups - w), p)
 
+    def zflip(step):
+        return (2 * ZED * w + 2 * (z + step * (1 - 2 * ((z // step) % 2))) + x, p)
+
     everyone = [sib, ypeer, diag, xpeer] + [zpeer(j) for j in range(1, ZED)] + [wpeer(j) for j in range(1, groups)]
 
+    arrivals = [
+        pltpu.make_async_copy(in_hbm, in_ref, a_sem.at[0]),
+        pltpu.make_async_copy(given_hbm, given_ref, a_sem.at[1]),
+    ]
+    for copy in arrivals:
+        copy.start()
     weight_copies = [
         pltpu.make_async_copy(src, dst, w_sem.at[i])
         for i, (src, dst) in enumerate(
@@ -132,16 +140,18 @@
             def _(j=j):
                 input_copies(j)[n].wait_send()
 
-    for n in range(2):
+    def send_inputs(n):
         for j in range(1, size):
             @pl.when((p + j) % size > 0)
-            def _(j=j, n=n):
+            def _(j=j):
                 input_copies(j)[n].start()
 
-    @pl.when(p > 0)
-    def _():
-        for copy in own_inputs():
-            copy.start()
+        @pl.when(p > 0)
+        def _():
+            own_inputs()[n].start()
+
+    arrivals[0].wait()
+    send_inputs(0)
 
     @pl.when(p == 0)
     def _():
@@ -223,7 +233,7 @@
                     pl.ds(pl.multiple_of(s * rows, rows), rows),
                     pl.ds(pl.multiple_of(u * feat + h * half, half), half),
                 ],
-                s_sem.at[c % STORES, h],
+                s_sem.at[h],
             )
             for h in range(2)
         ]
@@ -312,16 +322,10 @@
 
     def stage_s(c):
         copy_h(c).wait()
-
-        @pl.when(c >= STORES)
-        def _():
-            for copy in copy_s(c - STORES):
-                copy.wait()
-
         for copy in copy_s(c):
             copy.start()
 
-    ways = [[sib], [ypeer], [xpeer], [zpeer(j) for j in range(1, ZED)]]
+    ways = [[sib], [ypeer], [xpeer], [zflip(1)], [zflip(2)]]
     if groups > 1:
         ways.append([wpeer(j) for j in range(1, groups)])
     firsts = [sum(len(way) for way in ways[:i]) for i in range(len(ways))]
@@ -480,6 +484,7 @@
         return scale * (t - jnp.mean(t, axis=-1, keepdims=True) - norm * jnp.mean(t * norm, axis=-1, keepdims=True))
 
     def backward(i, grad):
+        pairs = BACKWARD_PAIRS[i]
         branch = grad.astype(BF16)
         right[rows_of(i), 0:feat] = branch
         if i == 0:
@@ -500,8 +505,8 @@
 
         def group(first_pair, carry):
             mid = seq // 2
-            for u in range(BACKWARD_PAIRS):
-                hp = first_pair * BACKWARD_PAIRS + u
+            for u in range(pairs):
+                hp = first_pair * pairs + u
                 lanes = pl.ds(pl.multiple_of(hp * half, half), half)
                 q2 = qkv[i, :, lanes]
                 do2 = dctx[:, lanes]
@@ -555,7 +560,7 @@
                 step(EARLY[1] + first_pair, 0)
             return carry
 
-        lax.fori_loop(0, feat // half // BACKWARD_PAIRS, group, 0)
+        lax.fori_loop(0, feat // half // pairs, group, 0)
         right[rows_of(i), QKV : QKV + feat] = dqt[...].T
         d_normed = None
         for j in range(3):
@@ -566,6 +571,8 @@
         return d_mixed + norm_back(state[i], d_normed, row(gain1_ref), 0, i == 1)
 
     wait_inputs(0)
+    arrivals[1].wait()
+    send_inputs(1)
     state[0] = x_ref[...].astype(F32)
     first = forward(0)
     state[1] = first.astype(BF16).astype(F32) + row(embed_ref)
@@ -586,9 +593,8 @@
     vec_part[5:8, :] = jnp.zeros((3, feat), F32)
     d_state = backward(0, d_carry.astype(BF16).astype(F32))
     grad_seq[...] = d_state.astype(BF16)
-    send_results(1)
-
-    begun = EARLY[1] + feat // half // BACKWARD_PAIRS
+
+    begun = EARLY[1] + feat // half // BACKWARD_PAIRS[0]
     vector_step(0)
 
     def late_step(t, carry):
@@ -597,6 +603,10 @@
             @pl.when(t == begun + 3 * i)
             def _(i=i):
                 vector_step(i)
+
+        @pl.when(t == chunks + offsets[1])
+        def _():
+            send_results(1)
 
         return carry
 
@@ -619,12 +629,8 @@
             for n, dst in enumerate((out_ref, gin_ref)):
                 pltpu.make_async_copy(dst.at[source - 1], dst.at[source - 1], o_rs.at[n, j - 1]).wait()
 
-    def finish(c, carry):
-        for copy in copy_s(c):
-            copy.wait()
-        return carry
-
-    lax.fori_loop(chunks - STORES, chunks, finish, 0)
+    for h in range(2):
+        pltpu.make_async_copy(full.at[:, h], full.at[:, h], s_sem.at[h]).wait()
 
 
 def run_block(inputs, cotangent, lengths, vectors, w_qkv, w_out, w_up, w_down, rows, lags, groups):
@@ -636,8 +642,8 @@
     chunks = units * (quarter // rows)
     piece = rows // ZED
     half = feat // 2
-    ways = 4 + (groups > 1)
-    landings = 6 + (groups - 1)
+    ways = 5 + (groups > 1)
+    landings = 5 + (groups - 1)
     more = max(groups - 1, 1)
     dma = pltpu.SemaphoreType.DMA
     local_block = jax.ShapeDtypeStruct((slots, block, feat), BF16)
@@ -651,9 +657,11 @@
             local_block,
             jax.ShapeDtypeStruct((8, feat), F32),
         ),
-        in_specs=[VMEM, VMEM, SMEM] + [VMEM] * 5 + [ANY] * 4,
+        in_specs=[ANY, ANY, SMEM] + [VMEM] * 5 + [ANY] * 4,
         out_specs=(ANY, VMEM, VMEM, VMEM),
         scratch_shapes=[
+            pltpu.VMEM(inputs.shape, BF16),
+            pltpu.VMEM(inputs.shape, BF16),
             pltpu.VMEM((seq, feat), BF16),
             pltpu.VMEM((seq, feat), BF16),
             pltpu.VMEM((seq, feat), BF16),
@@ -694,12 +702,12 @@
             pltpu.VMEM((SLOTS if groups > 1 else 1, more, piece, half), BF16),
             pltpu.VMEM((chunks, 2, rows, half), BF16),
             pltpu.VMEM((landings, 8, feat), F32),
-            dma((4,)), dma((2, slots)), dma((2, slots)),
+            dma((2,)), dma((4,)), dma((2, slots)), dma((2, slots)),
             dma((SLOTS,)), dma((SLOTS,)), dma((SLOTS,)), dma((SLOTS,)), dma((SLOTS,)), dma((SLOTS,)),
             dma((SLOTS, ZED - 1)), dma((SLOTS, ZED - 1)),
             dma((SLOTS if groups > 1 else 1, more)), dma((SLOTS if groups > 1 else 1, more)),
             dma((SLOTS, ZED - 1)), dma((SLOTS, ZED - 1)),
-            dma((SLOTS,)), dma((SLOTS,)), dma((STORES, 2)),
+            dma((SLOTS,)), dma((SLOTS,)), dma((2,)),
             dma((2, slots)), dma((2, slots)), dma((landings,)), dma((landings,)), dma((2,)),
         ],
         compiler_params=pltpu.CompilerParams(

time: 154 us -> 145 us (0.942)
  Pallas kernels: 153 us -> 144 us
    pallas_call x1, Pallas kernels: 147 us -> 138 us  [run_block(): pl.pallas_call(functools.partial(block_kernel, (rows, lags, groups)), out...]
where the time goes in v4:
time: 145 us
  Pallas kernels  144 us (99%)
    pallas_call x1, Pallas kernels, run_block(): pl.pallas_call(functools.partial(block_kernel, (rows, lags, groups)), out...  138 us
    pallas_call x1, Pallas kernels, run_finish(): pl.pallas_call(finish_kernel, out_shape=(jax.ShapeDtypeStruct(block_out.s...  5.96 us

profile of v4, /device:TPU:0, one launch (start us, length us, event | category | flops | bytes accessed | tf_op | source)
XLA Modules:
  0.0 144.6 jit_solution(11499684586163658651)
XLA Ops:
  0.6 137.8 %shard_map.203 = (bf16[192,9216]{1,0:T(8,128)(2,1)}, bf16[3,64,768]{2,1,0:T(8,128)(2,1)}, bf16[3,64,768]{2,1,0:T(8,128)(2,1)}, f32[8,768]{1,0:T(8,128)}) custom-call(bf16[3,64,768]{2,1,0:T(8,128)(2,1)} %in_hbm.1, bf16[3,64,768]{2,1,0:T(8,128)(2,1)} %given_hbm.1, s32[3]{0:T(128)} %len_ref.1, f32[768]{0:T(1024)} %gain1_ref.1, f32[768]{0:T(1024)} %shift1_ref.1, ...), custom_call_target="tpu_custom_call" | custom-call | tf_op jit(solution)/shard_map/pallas_call | solution.py:652
  138.5 6.0 %shard_map.204 = (bf16[3,64,768]{2,1,0:T(8,128)(2,1)}, bf16[3,64,768]{2,1,0:T(8,128)(2,1)}, f32[192,2304]{1,0:T(8,128)}, f32[192,768]{1,0:T(8,128)}, f32[192,307...) custom-call(bf16[192,9216]{1,0:T(8,128)(2,1)} %get-tuple-element.15., ...), custom_call_target="tpu_custom_call" | custom-call | tf_op jit(solution)/shard_map/pallas_call | solution.py:767

commit v5 on v4

--- a/solution.py
+++ b/solution.py
@@ -38,8 +38,9 @@
 ZED = 4
 SLOTS = 8
 ROWS = 64
-LAGS = (0, 1, 2, 2, 2, 2, 2, 2)
+LAGS = (0, 1, 2, 2, 2, 2, 2, 2, 2)
 EARLY = (3, 6)
+EARLY_CHUNKS = 12
 FORWARD_PAIRS = 6
 BACKWARD_PAIRS = (1, 6)
 
@@ -193,7 +194,20 @@
 
     def copy_x(c):
         return pltpu.make_async_remote_copy(
-            x_send.at[c % SLOTS], x_recv.at[c % SLOTS], x_ss.at[c % SLOTS], x_rs.at[c % SLOTS], device_id=xpeer, device_id_type=MESH
+            x_send.at[c % SLOTS, 0], x_recv.at[c % SLOTS, 0], x_ss.at[c % SLOTS], x_rs.at[c % SLOTS], device_id=xpeer, device_id_type=MESH
+        )
+
+    def early_copy_x(c):
+        return pltpu.make_async_remote_copy(
+            x_send.at[c % SLOTS], x_recv.at[c % SLOTS], x_ss.at[c % SLOTS], x_rs.at[c % SLOTS],
+            device_id=xpeer, device_id_type=MESH,
+        )
+
+    def early_copy_y(c):
+        cols = pl.ds(0, feat // 2)
+        return pltpu.make_async_remote_copy(
+            y_send.at[c % SLOTS, :, cols], y_recv.at[c % SLOTS, :, cols], y_ss.at[c % SLOTS], y_rs.at[c % SLOTS],
+            device_id=ypeer, device_id_type=MESH,
         )
 
     def part_of(k):
@@ -211,10 +225,12 @@
             device_id=wpeer(j), device_id_type=MESH,
         )
 
-    def copy_g(c, j):
-        place = full.at[c, x, part_of(z)]
+    def copy_g(c, n):
+        other = z + 2 - 4 * (z // 2)
+        place = full.at[c, x, part_of(other if n == 2 else z)]
         return pltpu.make_async_remote_copy(
-            place, place, g_ss.at[c % SLOTS, j - 1], g_rs.at[c % SLOTS, j - 1], device_id=zpeer(j), device_id_type=MESH
+            place, place, g_ss.at[c % SLOTS, n], g_rs.at[c % SLOTS, n],
+            device_id=zflip(2 if n == 0 else 1), device_id_type=MESH,
         )
 
     def copy_h(c):
@@ -272,19 +288,44 @@
 
         @pl.when(x == 0)
         def _():
-            x_send[c % SLOTS] = total[:, half:].astype(BF16)
-            x_keep[c % SLOTS] = total[:, :half]
+            x_send[c % SLOTS, 0] = total[:, half:].astype(BF16)
+            x_keep[c % SLOTS, 0] = total[:, :half]
 
         @pl.when(x == 1)
         def _():
-            x_send[c % SLOTS] = total[:, :half].astype(BF16)
-            x_keep[c % SLOTS] = total[:, half:]
+            x_send[c % SLOTS, 0] = total[:, :half].astype(BF16)
+            x_keep[c % SLOTS, 0] = total[:, half:]
 
         copy_x(c).start()
 
     def stage_z(c):
         copy_x(c).wait()
-        total = x_keep[c % SLOTS] + x_recv[c % SLOTS].astype(F32)
+        send_z(c, x_keep[c % SLOTS, 0] + x_recv[c % SLOTS, 0].astype(F32))
+
+    def early_x(c):
+        copy_d(c).wait()
+        half = feat // 2
+        sums = [own[c % 2, n] + d_recv[c % SLOTS, n].astype(F32) for n in range(2)]
+        for side in range(2):
+            @pl.when(x == side)
+            def _(side=side):
+                for n in range(2):
+                    x_send[c % SLOTS, n] = sums[n][:, (1 - side) * half : (2 - side) * half].astype(BF16)
+                    x_keep[c % SLOTS, n] = sums[n][:, side * half : (side + 1) * half]
+
+        early_copy_x(c).start()
+
+    def early_y(c):
+        early_copy_x(c).wait()
+        y_send[c % SLOTS, :, : feat // 2] = (x_keep[c % SLOTS, 0] + x_recv[c % SLOTS, 0].astype(F32)).astype(BF16)
+        early_copy_y(c).start()
+        x_keep[c % SLOTS, 1] += x_recv[c % SLOTS, 1].astype(F32)
+
+    def early_z(c):
+        early_copy_y(c).wait()
+        send_z(c, x_keep[c % SLOTS, 1] + y_recv[c % SLOTS, :, : feat // 2].astype(F32))
+
+    def send_z(c, total):
         z_send[c % SLOTS] = total.astype(BF16)
         for j in range(1, ZED):
             copy_z(c, j).start()
@@ -312,12 +353,16 @@
 
     def stage_g(c):
         full[c, x, part_of(z)] = (add_z(c) if groups == 1 else add_w(c)).astype(BF16)
-        for j in range(1, ZED):
-            copy_g(c, j).start()
+        copy_g(c, 0).start()
+        copy_g(c, 1).start()
+
+    def stage_g2(c):
+        copy_g(c, 0).wait()
+        copy_g(c, 2).start()
 
     def stage_h(c):
-        for j in range(1, ZED):
-            copy_g(c, j).wait()
+        copy_g(c, 1).wait()
+        copy_g(c, 2).wait()
         copy_h(c).start()
 
     def stage_s(c):
@@ -353,14 +398,24 @@
             for copy in vector_copies(i):
                 copy.start()
 
-    stages = [make, stage_y, stage_x, stage_z] + ([stage_w] if groups > 1 else []) + [stage_g, stage_h, stage_s]
+    stages = [make, stage_y, stage_x, stage_z] + ([stage_w] if groups > 1 else []) + [stage_g, stage_g2, stage_h, stage_s]
     offsets = [sum(lags[: i + 1]) for i in range(len(stages))]
+    early_stages = {1: early_x, 2: early_y, 3: early_z}
 
     def step(t, carry):
-        for stage, offset in zip(stages, offsets):
+        for i, (stage, offset) in enumerate(zip(stages, offsets)):
             c = t - offset
-
-            @pl.when((c >= 0) & (c < chunks))
+            present = (c >= 0) & (c < chunks)
+            if i in early_stages:
+                early = (c < EARLY_CHUNKS) & (c % 2 == 1)
+
+                @pl.when(present & early)
+                def _(stage=early_stages[i], c=c):
+                    stage(c)
+
+                present = present & ((c >= EARLY_CHUNKS) | (c % 2 == 0))
+
+            @pl.when(present)
             def _(stage=stage, c=c):
                 stage(c)
 
@@ -693,9 +748,9 @@
             pltpu.VMEM((SLOTS, rows, feat), BF16),
             pltpu.VMEM((SLOTS, rows, feat), F32),
             pltpu.VMEM((SLOTS, rows, feat), BF16),
-            pltpu.VMEM((SLOTS, rows, half), BF16),
-            pltpu.VMEM((SLOTS, rows, half), F32),
-            pltpu.VMEM((SLOTS, rows, half), BF16),
+            pltpu.VMEM((SLOTS, 2, rows, half), BF16),
+            pltpu.VMEM((SLOTS, 2, rows, half), F32),
+            pltpu.VMEM((SLOTS, 2, rows, half), BF16),
             pltpu.VMEM((SLOTS, rows, half), BF16),
             pltpu.VMEM((SLOTS, ZED - 1, piece, half), BF16),
             pltpu.VMEM((SLOTS if groups > 1 else 1, piece, half), BF16),
@@ -711,7 +766,7 @@
             dma((2, slots)), dma((2, slots)), dma((landings,)), dma((landings,)), dma((2,)),
         ],
         compiler_params=pltpu.CompilerParams(
-            collective_id=0, has_side_effects=True, vmem_limit_bytes=60 * 2**20
+            collective_id=0, has_side_effects=True, vmem_limit_bytes=61 * 2**20
         ),
     )(inputs, cotangent, lengths, *vectors, w_qkv, w_out, w_up, w_down)
 
@@ -789,7 +844,7 @@
     groups = lax.axis_size("dp") // (2 * ZED)
     vectors = (norm1_gain, norm1_shift, norm2_gain, norm2_shift, pass_embed)
     sums, block_out, input_grads, vec = run_block(
-        inputs, cotangent, lengths, vectors, w_qkv, w_out, w_up, w_down, ROWS, LAGS[: 7 + (groups > 1)], groups
+        inputs, cotangent, lengths, vectors, w_qkv, w_out, w_up, w_down, ROWS, LAGS[: 8 + (groups > 1)], groups
     )
     return run_finish(sums, block_out, input_grads, vec, ff)
 

time: 145 us -> 144 us (level)
  no operation moved by 1% of the time
where the time goes in v5:
time: 144 us
  Pallas kernels  143 us (99%)
    pallas_call x1, Pallas kernels, run_block(): pl.pallas_call(functools.partial(block_kernel, (rows, lags, groups)), out...  137 us
    pallas_call x1, Pallas kernels, run_finish(): pl.pallas_call(finish_kernel, out_shape=(jax.ShapeDtypeStruct(block_out.s...  5.96 us

profile of v5, /device:TPU:0, one launch (start us, length us, event | category | flops | bytes accessed | tf_op | source)
XLA Modules:
  0.0 144.2 jit_solution(15120187362796048799)
XLA Ops:
  0.6 137.4 %shard_map.203 = (bf16[192,9216]{1,0:T(8,128)(2,1)}, bf16[3,64,768]{2,1,0:T(8,128)(2,1)}, bf16[3,64,768]{2,1,0:T(8,128)(2,1)}, f32[8,768]{1,0:T(8,128)}) custom-call(bf16[3,64,768]{2,1,0:T(8,128)(2,1)} %in_hbm.1, bf16[3,64,768]{2,1,0:T(8,128)(2,1)} %given_hbm.1, s32[3]{0:T(128)} %len_ref.1, f32[768]{0:T(1024)} %gain1_ref.1, f32[768]{0:T(1024)} %shift1_ref.1, ...), custom_call_target="tpu_custom_call" | custom-call | tf_op jit(solution)/shard_map/pallas_call | solution.py:707
  138.0 6.0 %shard_map.204 = (bf16[3,64,768]{2,1,0:T(8,128)(2,1)}, bf16[3,64,768]{2,1,0:T(8,128)(2,1)}, f32[192,2304]{1,0:T(8,128)}, f32[192,768]{1,0:T(8,128)}, f32[192,307...) custom-call(bf16[192,9216]{1,0:T(8,128)(2,1)} %get-tuple-element.15., ...), custom_call_target="tpu_custom_call" | custom-call | tf_op jit(solution)/shard_map/pallas_call | solution.py:822
